TPU v7x, 32 devices: a whole 2x2x4 slice. The times are simulated.
32 devices in a mesh: expert: 8 (over z, core), seq: 4 (over y, x).
Axes of the slice: x: 2, y: 2, z: 4, core: 2. Of those that a mesh axis runs over, the one named last changes fastest.
Arguments:
- tokens: bfloat16 [8192, 1024], P(('expert', 'seq')), may hold values from -45 to 45
- cotangent: bfloat16 [8192, 1024], P(('expert', 'seq')), may hold values from -6 to 6
- expert_ids: int32 [8192, 2], P(('expert', 'seq')), may hold values from 0 to 7, all different within a row; in each aligned block of 256 rows (0 to 255, 256 to 511, ...) at most 160 rows name the same one
- segment_lengths: int32 [8, 13], P('expert'), may hold values from 1 to 409, 1024 in all within a row
- segment_parents: int32 [8, 13], P('expert'), may hold values from 0 to 11, as said below
- attention_gain: bfloat16 [1024], P(('expert', 'seq')), may hold values from 0.5 to 1.5
- query_weight: bfloat16 [1024, 1024], P(('expert', 'seq')), may hold values from -0.1875 to 0.1875
- key_weight: bfloat16 [1024, 1024], P(('expert', 'seq')), may hold values from -0.1875 to 0.1875
- value_weight: bfloat16 [1024, 1024], P(('expert', 'seq')), may hold values from -0.1875 to 0.1875
- output_weight: bfloat16 [1024, 1024], P(('expert', 'seq')), may hold values from -0.75 to 0.75
- bias_table: bfloat16 [512], P(('expert', 'seq')), may hold values from -4 to 4
- feedforward_gain: bfloat16 [1024], P(('expert', 'seq')), may hold values from 0.5 to 1.5
- router_weight: bfloat16 [1024, 8], P(('expert', 'seq')), may hold values from -0.1875 to 0.1875
- gate_weight: bfloat16 [8, 2816, 1024], P('expert', 'seq'), may hold values from -0.1875 to 0.1875
- up_weight: bfloat16 [8, 2816, 1024], P('expert', 'seq'), may hold values from -0.1875 to 0.1875
- down_weight: bfloat16 [8, 2816, 1024], P('expert', 'seq'), may hold values from -0.21875 to 0.21875
Outputs:
- layer_out: bfloat16 [8192, 1024], P(('expert', 'seq'))
- tokens_grad: float32 [8192, 1024], P(('expert', 'seq'))
- attention_gain_grad: float32 [1024], P(('expert', 'seq'))
- query_grad: float32 [1024, 1024], P(('expert', 'seq'))
- key_grad: float32 [1024, 1024], P(('expert', 'seq'))
- value_grad: float32 [1024, 1024], P(('expert', 'seq'))
- output_grad: float32 [1024, 1024], P(('expert', 'seq'))
- bias_table_grad: float32 [512], P(('expert', 'seq'))
- feedforward_gain_grad: float32 [1024], P(('expert', 'seq'))
- router_grad: float32 [1024, 8], P(('expert', 'seq'))
- gate_grad: float32 [8, 2816, 1024], P('expert', 'seq')
- up_grad: float32 [8, 2816, 1024], P('expert', 'seq')
- down_grad: float32 [8, 2816, 1024], P('expert', 'seq')
- root_mean_squares: float32 [2], replicated
Inputs may be any that keep to these rules, and one draw needn't show every extreme that they name: `expert_ids`: the two ids of a token differ. In the rows of one device no expert is named more than 2 * 80 times. `segment_lengths`: each tree's lengths sum to 1024. `segment_parents`: segment 0 is the root and its own parent; every other segment has a parent with a lower number; the last segment's parent is the one before it.
All inputs are finite; a program needn't handle non-finite values.
Results may differ from a plain program's by a relative error of at most 0.025.
Values may be sent and summed in bfloat16 or wider, within the bound.
A program may use at most 256 MiB of HBM per device.

v0:
```python
import math

import jax
import jax.numpy as jnp
from jax import lax
from jax.sharding import PartitionSpec as P

D = 1024
HEADS = 16
HDIM = 64
BUCKETS = 32
MAXDIST = 128


EPSILON = 1e-06
NEGATIVE = -1e30


def norm_factor(values):
    return lax.rsqrt(jnp.mean(values * values, axis=-1, keepdims=True) + EPSILON)


def gelu_tanh(values):
    return jax.nn.gelu(values, approximate=True)


def bucket_of(distance):
    exact_span = BUCKETS // 2
    above = jnp.zeros(distance.shape, jnp.int32)
    for number in range(exact_span):
        threshold = int(math.ceil(exact_span * (MAXDIST / exact_span) ** (number / exact_span)))
        above = above + (distance >= threshold).astype(jnp.int32)
    return jnp.where(distance < exact_span, distance, exact_span - 1 + above)


def tree_tables(lengths, parents):
    ordinal = jnp.arange(lengths.shape[0], dtype=jnp.int32)
    starts = jnp.cumsum(lengths) - lengths

    def chase(number, running):
        current, reaches = running
        current = jnp.sum(
            jnp.where(current[:, None] == ordinal[None, :], parents[None, :], 0), axis=1
        )
        reaches = jnp.maximum(reaches, (current[:, None] == ordinal[None, :]).astype(jnp.int32))
        return (current, reaches)

    begin = (ordinal, (ordinal[:, None] == ordinal[None, :]).astype(jnp.int32))
    unused, reaches = lax.fori_loop(0, lengths.shape[0], chase, begin)
    before = jnp.sum(reaches * lengths[None, :], axis=1) - lengths
    return (starts, before, reaches)


def token_info(token_rows, starts, before, reaches):
    ordinal = jnp.arange(starts.shape[0], dtype=jnp.int32)
    segment = jnp.sum((token_rows[:, None] >= starts[None, :]).astype(jnp.int32), axis=1) - 1
    member = segment[:, None] == ordinal[None, :]
    position = token_rows + jnp.sum(jnp.where(member, (before - starts)[None, :], 0), axis=1)
    lineage = jnp.sum(jnp.where(member[:, :, None], reaches[None, :, :], 0), axis=1)
    return (member.astype(jnp.float32), position, lineage.astype(jnp.float32))


def pair_terms(query_meta, key_meta, query_rows, key_rows, bias_grid):
    visible = jnp.dot(query_meta[2], key_meta[0].T, preferred_element_type=jnp.float32) > 0.5
    visible = visible & (key_rows[None, :] <= query_rows[:, None])
    distance = jnp.maximum(query_meta[1][:, None] - key_meta[1][None, :], 0)
    onehot = (
        bucket_of(distance)[:, :, None] == jnp.arange(BUCKETS, dtype=jnp.int32)[None, None, :]
    ).astype(jnp.bfloat16)
    pair_bias = jnp.einsum("qkb,bh->hqk", onehot, bias_grid, preferred_element_type=jnp.float32)
    return (visible, onehot, pair_bias)


def masked_scores(query_block, key_block, visible, pair_bias):
    scores = (
        jnp.einsum("qhd,khd->hqk", query_block, key_block, preferred_element_type=jnp.float32)
        * HDIM ** (-0.5)
        + pair_bias
    )
    return jnp.where(visible[None], scores, NEGATIVE)


def per_device(
    tokens,
    cotangent,
    expert_ids,
    segment_lengths,
    segment_parents,
    attention_gain,
    query_weight,
    key_weight,
    value_weight,
    output_weight,
    bias_table,
    feedforward_gain,
    router_weight,
    gate_weight,
    up_weight,
    down_weight,
):
    seq_count = lax.axis_size("seq")
    seq_place = lax.axis_index("seq")
    all_count = lax.axis_size("expert") * seq_count
    row_count = tokens.shape[0]
    experts = lax.axis_size("expert") * gate_weight.shape[0]
    capacity = 10 * row_count // (4 * experts)
    score_scale = HDIM ** (-0.5)
    gathered = (
        lax.all_gather(attention_gain, ("expert", "seq"), axis=0, tiled=True),
        lax.all_gather(query_weight, ("expert", "seq"), axis=0, tiled=True),
        lax.all_gather(key_weight, ("expert", "seq"), axis=0, tiled=True),
        lax.all_gather(value_weight, ("expert", "seq"), axis=0, tiled=True),
        lax.all_gather(output_weight, ("expert", "seq"), axis=0, tiled=True),
        lax.all_gather(bias_table, ("expert", "seq"), axis=0, tiled=True),
        lax.all_gather(feedforward_gain, ("expert", "seq"), axis=0, tiled=True),
        lax.all_gather(router_weight, ("expert", "seq"), axis=0, tiled=True),
    )
    gain_one, query_full, key_full, value_full, output_full, bias_flat, gain_two, router_full = (
        gathered
    )
    bias_grid = bias_flat.reshape(BUCKETS, HEADS)
    starts, before, reaches = tree_tables(segment_lengths[0], segment_parents[0])
    own_rows = seq_place * row_count + jnp.arange(row_count, dtype=jnp.int32)
    own_meta = token_info(own_rows, starts, before, reaches)
    tokens_float = tokens.astype(jnp.float32)
    scale_one = norm_factor(tokens_float)
    unit_one = tokens_float * scale_one
    normed_one = (unit_one * gain_one.astype(jnp.float32)).astype(jnp.bfloat16)
    queries = (
        jnp.dot(normed_one, query_full, preferred_element_type=jnp.float32)
        .astype(jnp.bfloat16)
        .reshape(row_count, HEADS, HDIM)
    )
    keys_own = (
        jnp.dot(normed_one, key_full, preferred_element_type=jnp.float32)
        .astype(jnp.bfloat16)
        .reshape(row_count, HEADS, HDIM)
    )
    values_own = (
        jnp.dot(normed_one, value_full, preferred_element_type=jnp.float32)
        .astype(jnp.bfloat16)
        .reshape(row_count, HEADS, HDIM)
    )
    row_peak = jnp.full((HEADS, row_count), NEGATIVE, jnp.float32)
    key_piece = lax.all_gather(keys_own, "seq", axis=0, tiled=True)
    value_piece = lax.all_gather(values_own, "seq", axis=0, tiled=True)
    key_rows = jnp.arange(key_piece.shape[0], dtype=jnp.int32)
    visible, onehot, pair_bias = pair_terms(
        own_meta, token_info(key_rows, starts, before, reaches), own_rows, key_rows, bias_grid
    )
    scores = masked_scores(queries, key_piece, visible, pair_bias)
    new_peak = jnp.maximum(row_peak, jnp.max(scores, axis=-1))
    expo = jnp.exp(scores - new_peak[:, :, None])
    row_total = jnp.sum(expo, axis=-1)
    summed = jnp.einsum(
        "hqk,khd->qhd", expo.astype(jnp.bfloat16), value_piece, preferred_element_type=jnp.float32
    )
    row_peak, row_total, summed = (new_peak, row_total, summed)
    log_total = row_peak + jnp.log(row_total)
    attended_float = summed / jnp.transpose(row_total)[:, :, None]
    attended = attended_float.astype(jnp.bfloat16).reshape(row_count, D)
    residual = tokens_float + jnp.dot(attended, output_full, preferred_element_type=jnp.float32)
    scale_two = norm_factor(residual)
    unit_two = residual * scale_two
    normed_two = (unit_two * gain_two.astype(jnp.float32)).astype(jnp.bfloat16)
    router_prob = jax.nn.softmax(
        jnp.dot(normed_two, router_full, preferred_element_type=jnp.float32), axis=-1
    )
    pick_hot = (
        expert_ids[:, :, None] == jnp.arange(experts, dtype=jnp.int32)[None, None, :]
    ).astype(jnp.float32)
    chosen = jnp.sum(pick_hot * router_prob[:, None, :], axis=2)
    chosen_total = jnp.sum(chosen, axis=1, keepdims=True)
    gate_shares = chosen / chosen_total
    hot_int = pick_hot.astype(jnp.int32).reshape(row_count * 2, experts)
    earlier = jnp.cumsum(hot_int, axis=0) - hot_int
    slot_number = jnp.sum(earlier * hot_int, axis=1).reshape(row_count, 2)
    kept_copy = slot_number < capacity
    kept_float = kept_copy.astype(jnp.float32)
    target = jnp.where(kept_copy, expert_ids * capacity + slot_number, experts * capacity)
    copy_ids = jnp.arange(row_count * 2, dtype=jnp.int32)
    slot_copy = (
        jnp.full((experts * capacity + 1,), row_count * 2, jnp.int32)
        .at[target.reshape(-1)]
        .set(copy_ids)[: experts * capacity]
    )
    fetch_index = jnp.minimum(target, experts * capacity - 1).reshape(-1)
    token_of_slot = jnp.where(slot_copy < row_count * 2, slot_copy // 2, row_count)
    padded = jnp.concatenate([normed_two, jnp.zeros((1, D), jnp.bfloat16)], axis=0)
    send_rows = padded[token_of_slot].reshape(experts, capacity, D)
    expert_in = lax.all_to_all(send_rows, "expert", split_axis=0, concat_axis=1, tiled=True)[0]
    gate_piece = lax.all_gather(gate_weight, "seq", axis=1, tiled=True)
    up_piece = lax.all_gather(up_weight, "seq", axis=1, tiled=True)
    down_piece = lax.all_gather(down_weight, "seq", axis=1, tiled=True)
    gate_pre = jnp.einsum("rd,fd->rf", expert_in, gate_piece[0], preferred_element_type=jnp.float32)
    up_pre = jnp.einsum("rd,fd->rf", expert_in, up_piece[0], preferred_element_type=jnp.float32)
    active = (gelu_tanh(gate_pre) * up_pre).astype(jnp.bfloat16)
    expert_sum = jnp.dot(active, down_piece[0], preferred_element_type=jnp.float32)
    returned = lax.all_to_all(
        expert_sum.astype(jnp.bfloat16)[None], "expert", split_axis=1, concat_axis=0, tiled=True
    )
    picked = (
        returned.reshape(experts * capacity, D)[fetch_index]
        .reshape(row_count, 2, D)
        .astype(jnp.float32)
    )
    weighted = gate_shares * kept_float
    mixture = jnp.sum(weighted[:, :, None] * picked, axis=1)
    layer_out = (residual + mixture).astype(jnp.bfloat16)
    local_sums = jnp.stack([jnp.sum(residual * residual), jnp.sum(mixture * mixture)])
    again = (
        lax.all_gather(attention_gain, ("expert", "seq"), axis=0, tiled=True),
        lax.all_gather(query_weight, ("expert", "seq"), axis=0, tiled=True),
        lax.all_gather(key_weight, ("expert", "seq"), axis=0, tiled=True),
        lax.all_gather(value_weight, ("expert", "seq"), axis=0, tiled=True),
        lax.all_gather(output_weight, ("expert", "seq"), axis=0, tiled=True),
        lax.all_gather(bias_table, ("expert", "seq"), axis=0, tiled=True),
        lax.all_gather(feedforward_gain, ("expert", "seq"), axis=0, tiled=True),
        lax.all_gather(router_weight, ("expert", "seq"), axis=0, tiled=True),
    )
    gain_one, query_full, key_full, value_full, output_full, bias_flat, gain_two, router_full = (
        again
    )
    bias_grid = bias_flat.reshape(BUCKETS, HEADS)
    grad_out = cotangent.astype(jnp.float32)
    copy_grad = (
        (weighted[:, :, None] * grad_out[:, None, :]).astype(jnp.bfloat16).reshape(row_count * 2, D)
    )
    copy_padded = jnp.concatenate([copy_grad, jnp.zeros((1, D), jnp.bfloat16)], axis=0)
    grad_send = copy_padded[slot_copy].reshape(experts, capacity, D)
    grad_in = lax.all_to_all(grad_send, "expert", split_axis=0, concat_axis=1, tiled=True)[0]
    gate_piece = lax.all_gather(gate_weight, "seq", axis=1, tiled=True)
    up_piece = lax.all_gather(up_weight, "seq", axis=1, tiled=True)
    down_piece = lax.all_gather(down_weight, "seq", axis=1, tiled=True)
    gate_pre = jnp.einsum("rd,fd->rf", expert_in, gate_piece[0], preferred_element_type=jnp.float32)
    up_pre = jnp.einsum("rd,fd->rf", expert_in, up_piece[0], preferred_element_type=jnp.float32)
    gelu_out, gelu_pull = jax.vjp(gelu_tanh, gate_pre)
    act_grad = jnp.einsum("rd,fd->rf", grad_in, down_piece[0], preferred_element_type=jnp.float32)
    gate_back = gelu_pull(act_grad * up_pre)[0].astype(jnp.bfloat16)
    up_back = (act_grad * gelu_out).astype(jnp.bfloat16)
    input_grad = jnp.dot(gate_back, gate_piece[0], preferred_element_type=jnp.float32) + jnp.dot(
        up_back, up_piece[0], preferred_element_type=jnp.float32
    )
    active = (gelu_out * up_pre).astype(jnp.bfloat16)
    input_grad, gate_backs, up_backs, actives = (input_grad, gate_back, up_back, active)
    grad_back = lax.all_to_all(
        input_grad.astype(jnp.bfloat16)[None], "expert", split_axis=1, concat_axis=0, tiled=True
    )
    expert_back = (
        grad_back.reshape(experts * capacity, D)[fetch_index]
        .reshape(row_count, 2, D)
        .astype(jnp.float32)
    )
    normed_two_grad = jnp.sum(expert_back * kept_float[:, :, None], axis=1)
    expert_grads = lax.psum_scatter(
        jnp.stack(
            [
                jnp.einsum("rf,rd->fd", gate_backs, expert_in, preferred_element_type=jnp.float32),
                jnp.einsum("rf,rd->fd", up_backs, expert_in, preferred_element_type=jnp.float32),
                jnp.einsum("rf,rd->fd", actives, grad_in, preferred_element_type=jnp.float32),
            ],
            axis=1,
        ).astype(jnp.bfloat16),
        "seq",
        scatter_dimension=0,
        tiled=True,
    ).astype(jnp.float32)
    share_grad = jnp.sum(grad_out[:, None, :] * picked, axis=2) * kept_float
    chosen_grad = (
        share_grad - jnp.sum(gate_shares * share_grad, axis=1, keepdims=True)
    ) / chosen_total
    prob_grad = jnp.sum(pick_hot * chosen_grad[:, :, None], axis=1)
    logit_grad = router_prob * (prob_grad - jnp.sum(router_prob * prob_grad, axis=1, keepdims=True))
    router_float = router_full.astype(jnp.float32)
    router_term = jnp.einsum(
        "rd,re->de", normed_two.astype(jnp.float32), logit_grad, precision=lax.Precision.HIGHEST
    )
    normed_two_grad = normed_two_grad + jnp.einsum(
        "re,de->rd", logit_grad, router_float, precision=lax.Precision.HIGHEST
    )
    gain_two_term = jnp.sum(normed_two_grad * unit_two, axis=0)
    unit_grad_two = normed_two_grad * gain_two.astype(jnp.float32)
    residual_grad = grad_out + scale_two * (
        unit_grad_two - unit_two * jnp.mean(unit_grad_two * unit_two, axis=-1, keepdims=True)
    )
    attention_out_grad = residual_grad.astype(jnp.bfloat16)
    output_term = jnp.einsum(
        "rd,re->de", attended, attention_out_grad, preferred_element_type=jnp.float32
    )
    attended_grad = (
        jnp.einsum("re,de->rd", attention_out_grad, output_full, preferred_element_type=jnp.float32)
        .astype(jnp.bfloat16)
        .reshape(row_count, HEADS, HDIM)
    )
    row_delta = jnp.transpose(jnp.sum(attended_grad.astype(jnp.float32) * attended_float, axis=-1))
    total_all, delta_all = (
        lax.all_gather(log_total, "seq", axis=1, tiled=True),
        lax.all_gather(row_delta, "seq", axis=1, tiled=True),
    )
    key_piece = lax.all_gather(keys_own, "seq", axis=0, tiled=True)
    value_piece = lax.all_gather(values_own, "seq", axis=0, tiled=True)
    key_rows = jnp.arange(key_piece.shape[0], dtype=jnp.int32)
    visible, onehot, pair_bias = pair_terms(
        own_meta, token_info(key_rows, starts, before, reaches), own_rows, key_rows, bias_grid
    )
    scores = masked_scores(queries, key_piece, visible, pair_bias)
    soft_weights = jnp.exp(scores - log_total[:, :, None])
    dprob = jnp.einsum(
        "qhd,khd->hqk", attended_grad, value_piece, preferred_element_type=jnp.float32
    )
    score_grad = (soft_weights * (dprob - row_delta[:, :, None])).astype(jnp.bfloat16)
    query_acc = jnp.einsum(
        "hqk,khd->qhd", score_grad, key_piece, preferred_element_type=jnp.float32
    )
    bias_acc = jnp.einsum("qkb,hqk->bh", onehot, score_grad, preferred_element_type=jnp.float32)
    query_acc, bias_acc = (query_acc, bias_acc)
    query_piece = lax.all_gather(queries, "seq", axis=0, tiled=True)
    grad_piece = lax.all_gather(attended_grad, "seq", axis=0, tiled=True)
    piece_rows = query_piece.shape[0]
    query_rows = jnp.arange(piece_rows, dtype=jnp.int32)
    visible, onehot, pair_bias = pair_terms(
        token_info(query_rows, starts, before, reaches), own_meta, query_rows, own_rows, bias_grid
    )
    scores = masked_scores(query_piece, keys_own, visible, pair_bias)
    soft_weights = jnp.exp(scores - total_all[:, :, None])
    value_acc = jnp.einsum(
        "hqk,qhd->khd",
        soft_weights.astype(jnp.bfloat16),
        grad_piece,
        preferred_element_type=jnp.float32,
    )
    dprob = jnp.einsum("qhd,khd->hqk", grad_piece, values_own, preferred_element_type=jnp.float32)
    score_grad = (soft_weights * (dprob - delta_all[:, :, None])).astype(jnp.bfloat16)
    key_acc = jnp.einsum(
        "hqk,qhd->khd", score_grad, query_piece, preferred_element_type=jnp.float32
    )
    key_acc, value_acc = (key_acc, value_acc)
    query_back = (query_acc * score_scale).astype(jnp.bfloat16).reshape(row_count, D)
    key_back = (key_acc * score_scale).astype(jnp.bfloat16).reshape(row_count, D)
    value_back = value_acc.astype(jnp.bfloat16).reshape(row_count, D)
    query_term = jnp.einsum("rd,re->de", normed_one, query_back, preferred_element_type=jnp.float32)
    key_term = jnp.einsum("rd,re->de", normed_one, key_back, preferred_element_type=jnp.float32)
    value_term = jnp.einsum("rd,re->de", normed_one, value_back, preferred_element_type=jnp.float32)
    normed_one_grad = jnp.einsum(
        "re,de->rd", query_back, query_full, preferred_element_type=jnp.float32
    )
    normed_one_grad = normed_one_grad + jnp.einsum(
        "re,de->rd", key_back, key_full, preferred_element_type=jnp.float32
    )
    normed_one_grad = normed_one_grad + jnp.einsum(
        "re,de->rd", value_back, value_full, preferred_element_type=jnp.float32
    )
    gain_one_term = jnp.sum(normed_one_grad * unit_one, axis=0)
    unit_grad_one = normed_one_grad * gain_one.astype(jnp.float32)
    tokens_grad = residual_grad + scale_one * (
        unit_grad_one - unit_one * jnp.mean(unit_grad_one * unit_one, axis=-1, keepdims=True)
    )
    stats_term = jnp.broadcast_to(local_sums[None, :], (all_count, 2))
    reduced = (
        lax.psum_scatter(gain_one_term, ("expert", "seq"), scatter_dimension=0, tiled=True),
        lax.psum_scatter(query_term, ("expert", "seq"), scatter_dimension=0, tiled=True),
        lax.psum_scatter(key_term, ("expert", "seq"), scatter_dimension=0, tiled=True),
        lax.psum_scatter(value_term, ("expert", "seq"), scatter_dimension=0, tiled=True),
        lax.psum_scatter(output_term, ("expert", "seq"), scatter_dimension=0, tiled=True),
        lax.psum_scatter(
            bias_acc.reshape(BUCKETS * HEADS), ("expert", "seq"), scatter_dimension=0, tiled=True
        ),
        lax.psum_scatter(gain_two_term, ("expert", "seq"), scatter_dimension=0, tiled=True),
        lax.psum_scatter(router_term, ("expert", "seq"), scatter_dimension=0, tiled=True),
        lax.psum_scatter(stats_term, ("expert", "seq"), scatter_dimension=0, tiled=True),
    )
    roots = jnp.sqrt(reduced[8][0] / (row_count * all_count * D))
    return (
        layer_out,
        tokens_grad,
        reduced[0],
        reduced[1],
        reduced[2],
        reduced[3],
        reduced[4],
        reduced[5],
        reduced[6],
        reduced[7],
        expert_grads[None, :, 0, :],
        expert_grads[None, :, 1, :],
        expert_grads[None, :, 2, :],
        roots,
    )


def solution(mesh):
    return jax.shard_map(
        per_device,
        mesh=mesh,
        in_specs=(
            P(("expert", "seq"), None),
            P(("expert", "seq"), None),
            P(("expert", "seq"), None),
            P("expert", None),
            P("expert", None),
            P(("expert", "seq")),
            P(("expert", "seq"), None),
            P(("expert", "seq"), None),
            P(("expert", "seq"), None),
            P(("expert", "seq"), None),
            P(("expert", "seq")),
            P(("expert", "seq")),
            P(("expert", "seq"), None),
            P("expert", "seq", None),
            P("expert", "seq", None),
            P("expert", "seq", None),
        ),
        out_specs=(
            P(("expert", "seq"), None),
            P(("expert", "seq"), None),
            P(("expert", "seq")),
            P(("expert", "seq"), None),
            P(("expert", "seq"), None),
            P(("expert", "seq"), None),
            P(("expert", "seq"), None),
            P(("expert", "seq")),
            P(("expert", "seq")),
            P(("expert", "seq"), None),
            P("expert", "seq", None),
            P("expert", "seq", None),
            P("expert", "seq", None),
            P(),
        ),
        check_vma=False,
    )
```

profile of v0, /device:TPU:0, one launch (start us, length us, event | category | flops | bytes accessed | tf_op | source)
XLA Modules:
  0.0 1570.7 jit_solution(5163732976471823254)
XLA Ops:
  12.0 42.1 %all-reduce.10 = (bf16[1024]{0:T(1024)(128)(2,1)S(1)}, bf16[512]{0:T(512)(128)(2,1)S(1)}, bf16[1024]{0:T(1024)(128)(2,1)S(1)}) all-reduce(bf16[1024]{0:T(1024)(128)(2,1)S(1)} %dynamic-update-slice, bf16[512]{0:T(512)(128)(2,1)S(1)} %dynamic-update-slice.1, ...), channel_id=1, replica_groups=mesh['expert'=8,'seq'=4] {'expert','seq'}, use_global_device_ids=true, to_apply=%add.2 | all-reduce | flops 2560 | bytes 10240
  55.4 14.7 all-gather.19.cloned.1.call-done
  73.7 54.5 %all-gather.13.cloned.1.call-done = bf16[1024,1024]{1,0:T(8,128)(2,1)} async-done(((bf16[32,1024]{1,0:T(8,128)(2,1)}), bf16[1024,1024]{1,0:T(8,128)(2,1)}) %all-gather.13.cloned.1.call-update) | async-done | bytes 2097168 | tf_op jit(solution)/shard_map/all_gather | solution.py:112
  154.2 46.6 %copy.130 = pred[256,1024,32]{1,2,0:T(32,128)(4,1)} copy(pred[256,1024,32]{0,2,1:T(32,128)(4,1)} %iota_compare_fusion.3) | data formatting | bytes 16777216 | tf_op jit(solution)/shard_map/eq | solution.py:68
  201.4 67.3 %all-gather = bf16[32,32,8]{1,2,0:T(8,128)(2,1)S(1)} all-gather(bf16[1,32,8]{1,2,0:T(8,128)(2,1)S(1)} %bitcast.195), channel_id=1, replica_groups=mesh['expert'=8,'seq'=4] {'expert','seq'}, dimensions={0}, use_global_device_ids=true | all-gather | bytes 16896 | tf_op jit(solution)/shard_map/all_gather | solution.py:116
  271.7 10.2 fusion.111
  284.6 22.1 %fusion.138 = (f32[16,256]{1,0:T(8,128)S(1)}, f32[16,256,1024]{2,1,0:T(8,128)}) fusion(f32[16,256,1024]{2,0,1:T(8,128)} %fusion.111, bf16[256,16,64]{0,2,1:T(8,128)(2,1)S(1)} %bitcast.171, bf16[1024,16,64]{0,2,1:T(8,128)(2,1)} %all-gather.21.cloned.1.call-done, pred[256,1024]{1,0:T(8,128)(4,1)S(1)} %fusion.59), kind=kOutput, calls=%fused_computation.238 | convolution fusion | flops 553644032 | bytes 36454400 | tf_op jit(solution)/shard_map/qhd,khd->hqk/dot_general | solution.py:76
  314.5 9.2 fusion.139
  341.1 28.7 %all-to-all-done.2 = bf16[8,80,1024]{2,1,0:T(8,128)(2,1)} async-done(((bf16[8,80,1024]{2,1,0:T(8,128)(2,1)}), bf16[8,80,1024]{2,1,0:T(8,128)(2,1)}, u32[]{:S(2)}, u32[]{:S(2)}) %all-to-all-start.2) | async-done | bytes 1310752 | tf_op jit(solution)/shard_map/all_to_all | solution.py:231
  373.4 12.1 all-gather.29.cloned.1.call-done
  385.5 10.3 fusion.22
  395.8 57.3 %all-gather.27.cloned.1.call-done = bf16[1,2816,1024]{2,1,0:T(8,128)(2,1)} async-done(((bf16[1,704,1024]{2,1,0:T(8,128)(2,1)}), bf16[1,2816,1024]{2,1,0:T(8,128)(2,1)}) %all-gather.27.cloned.1.call-update) | async-done | bytes 5767184 | tf_op jit(solution)/shard_map/all_gather | solution.py:193
  453.2 9.1 fusion.28
  462.3 58.5 %all-gather.25.cloned.1.call-done = bf16[1,2816,1024]{2,1,0:T(8,128)(2,1)} async-done(((bf16[1,704,1024]{2,1,0:T(8,128)(2,1)}), bf16[1,2816,1024]{2,1,0:T(8,128)(2,1)}) %all-gather.25.cloned.1.call-update) | async-done | bytes 5767184 | tf_op jit(solution)/shard_map/all_gather | solution.py:192
  520.8 17.2 %fusion.21 = (bf16[640,2816]{1,0:T(8,128)(2,1)}, bf16[640,2816]{1,0:T(8,128)(2,1)}, bf16[640,2816]{1,0:T(8,128)(2,1)S(1)}) fusion(f32[640,2816]{1,0:T(8,128)} %fusion.22, f32[640,2816]{1,0:T(8,128)} %fusion.28, bf16[640,1024]{1,0:T(8,128)(2,1)S(1)} %bitcast.188, bf16[1,2816,1024]{2,1,0:T(8,128)(2,1)} %all-gather.25.cloned.1.call-done), kind=kOutput, calls=%fused_computation.38 | convolution fusion | flops 3737845760 | bytes 32309248 | tf_op jit(solution)/shard_map/rd,fd->rf/dot_general | solution.py:195
  549.9 9.8 reduce.7
  583.3 10.1 reduce.8
  619.2 15.7 all-to-all-done.3
  664.4 9.7 convert_bitcast_fusion
  688.8 14.2 pad_maximum_fusion
  704.5 8.9 multiply_convert_fusion.1
  725.0 8.9 fusion.2
  742.6 24.2 %fusion.5 = f32[16,1024,256]{2,1,0:T(8,128)} fusion(f32[16,1024,256]{2,0,1:T(8,128)} %fusion.2, bf16[1024,16,64]{0,2,1:T(8,128)(2,1)} %all-gather.31.cloned.1.call-done, bf16[256,16,64]{0,2,1:T(8,128)(2,1)S(1)} %bitcast.176, f32[16,1024]{1,0:T(8,128)S(1)} %all_gather.78, pred[1024,256]{1,0:T(8,128)(4,1)S(1)} %fusion.60), kind=kOutput, calls=%fused_computation.17 | convolution fusion | flops 553648128 | bytes 36503552 | tf_op jit(solution)/shard_map/qhd,khd->hqk/dot_general | solution.py:76
  774.3 9.5 fusion.54
  797.8 12.7 copy.148
  822.3 11.7 reduce-scatter.19.cloned.1.call-done
  840.1 37.9 %all-reduce.9 = (f32[1024]{0:T(1024)S(1)}, f32[512]{0:T(512)S(1)}, f32[1024]{0:T(1024)S(1)}, f32[32,2]{1,0:T(8,128)S(1)}) all-reduce(f32[1024]{0:T(1024)S(1)} %get-tuple-element.73, f32[512]{0:T(512)S(1)} %reshape.572, f32[1024]{0:T(1024)S(1)} %get-tuple-element.69, ...), channel_id=2, replica_groups=mesh['expert'=8,'seq'=4] {'expert','seq'}, use_global_device_ids=true, to_apply=%region_33.34.clone | all-reduce | flops 2624 | bytes 20992
  882.8 110.0 %reduce-scatter.17.cloned.1.call-done = bf16[704,3,1024]{2,0,1:T(8,128)(2,1)} async-done(((bf16[2816,3,1024]{2,0,1:T(8,128)(2,1)}), bf16[704,3,1024]{2,0,1:T(8,128)(2,1)}) %reduce-scatter.17.cloned.1.call-update) | async-done | bytes 4325392 | tf_op jit(solution)/shard_map/reduce_scatter | solution.py:255
  999.8 137.2 %reduce-scatter.9.cloned.1.call-done = f32[32,1024]{1,0:T(8,128)} async-done(((f32[1024,1024]{1,0:T(8,128)}), f32[32,1024]{1,0:T(8,128)}) %reduce-scatter.9.cloned.1.call-update) | async-done | bytes 131088 | tf_op jit(solution)/shard_map/reduce_scatter | solution.py:361
  1137.0 142.3 %reduce-scatter.15.cloned.1.call-done = f32[32,1024]{1,0:T(8,128)} async-done(((f32[1024,1024]{1,0:T(8,128)}), f32[32,1024]{1,0:T(8,128)}) %reduce-scatter.15.cloned.1.call-update) | async-done | bytes 131088 | tf_op jit(solution)/shard_map/reduce_scatter | solution.py:364
  1279.3 142.1 %reduce-scatter.11.cloned.1.call-done = f32[32,1024]{1,0:T(8,128)} async-done(((f32[1024,1024]{1,0:T(8,128)}), f32[32,1024]{1,0:T(8,128)}) %reduce-scatter.11.cloned.1.call-update) | async-done | bytes 131088 | tf_op jit(solution)/shard_map/reduce_scatter | solution.py:362
  1421.4 142.5 %reduce-scatter.13.cloned.1.call-done = f32[32,1024]{1,0:T(8,128)} async-done(((f32[1024,1024]{1,0:T(8,128)}), f32[32,1024]{1,0:T(8,128)}) %reduce-scatter.13.cloned.1.call-update) | async-done | bytes 131088 | tf_op jit(solution)/shard_map/reduce_scatter | solution.py:363
  (388 shorter events, 251.1 us)
Async XLA Ops:
  7.2 121.0 %copy-start.1 = (bf16[256,1024]{1,0:T(8,128)(2,1)S(1)}, bf16[256,1024]{1,0:T(8,128)(2,1)}, u32[]{:S(2)}) copy-start(bf16[256,1024]{1,0:T(8,128)(2,1)} %param.18) | copy-start | bytes 1572868
  7.2 62.9 %all-gather.19.cloned.1.call-start = ((), (), s32[]{:S(2)}) async-start(), calls=%async_computation.13 | async-start | bytes 2162688 | tf_op jit(solution)/shard_map/all_gather | solution.py:111
  7.9 120.3 %all-gather.13.cloned.1.call-start = ((), (), s32[]{:S(2)}) async-start(), calls=%async_computation.10 | async-start | bytes 2162688 | tf_op jit(solution)/shard_map/all_gather | solution.py:112
  8.7 273.3 %all-gather.17.cloned.1.call-start = ((), (), s32[]{:S(2)}) async-start(), calls=%async_computation.12 | async-start | bytes 2162688 | tf_op jit(solution)/shard_map/all_gather | solution.py:110
  9.4 275.2 %all-gather.21.cloned.1.call-start = ((), (), s32[]{:S(2)}) async-start(), calls=%async_computation.14 | async-start | bytes 2621440 | tf_op jit(solution)/shard_map/all_gather | solution.py:145
  54.1 227.9 %copy-start.26 = (f32[1024]{0:T(1024)}, f32[1024]{0:T(1024)S(1)}, u32[]{:S(2)}) copy-start(f32[1024]{0:T(1024)S(1)} %convert_element_type.406) | copy-start | bytes 12292
  55.4 226.6 %copy-start.49 = (f32[256]{0:T(256)}, f32[256]{0:T(256)S(1)}, u32[]{:S(2)}) copy-start(f32[256]{0:T(256)S(1)} %add_rsqrt_fusion.1) | copy-start | bytes 3076
  73.7 60.8 %copy-start.51 = (s32[256,2]{0,1:T(2,128)S(1)}, s32[256,2]{0,1:T(2,128)}, u32[]{:S(2)}) copy-start(s32[256,2]{0,1:T(2,128)} %param.20) | copy-start | bytes 6148
  73.7 61.2 %copy-start.10 = (bf16[256,1024]{1,0:T(8,128)(2,1)S(1)}, bf16[256,1024]{1,0:T(8,128)(2,1)}, u32[]{:S(2)}) copy-start(bf16[256,1024]{1,0:T(8,128)(2,1)} %param.19) | copy-start | bytes 1572868
  73.7 240.8 %all-gather.15.cloned.1.call-start = ((), (), s32[]{:S(2)}) async-start(), calls=%async_computation.11 | async-start | bytes 2621440 | tf_op jit(solution)/shard_map/all_gather | solution.py:146
  131.6 192.2 %all-gather.23.cloned.1.call-start = ((), (), s32[]{:S(2)}) async-start(), calls=%async_computation.15 | async-start | bytes 2162688 | tf_op jit(solution)/shard_map/all_gather | solution.py:113
  132.2 253.3 %all-gather.29.cloned.1.call-start = ((), (), s32[]{:S(2)}) async-start(), calls=%async_computation.18 | async-start | bytes 7208960 | tf_op jit(solution)/shard_map/all_gather | solution.py:194
  132.9 320.2 %all-gather.27.cloned.1.call-start = ((), (), s32[]{:S(2)}) async-start(), calls=%async_computation.17 | async-start | bytes 7208960 | tf_op jit(solution)/shard_map/all_gather | solution.py:193
  133.7 387.1 %all-gather.25.cloned.1.call-start = ((), (), s32[]{:S(2)}) async-start(), calls=%async_computation.16 | async-start | bytes 7208960 | tf_op jit(solution)/shard_map/all_gather | solution.py:192
  139.6 465.1 %copy-start.41 = (s32[256,2]{0,1:T(2,128)}, s32[256,2]{0,1:T(2,128)S(1)}, u32[]{:S(2)}) copy-start(s32[256,2]{0,1:T(2,128)S(1)} %copy.134) | copy-start | bytes 6148
  143.3 57.6 %copy-start.24 = (s32[13,13]{1,0:T(8,128)}, s32[13,13]{1,0:T(8,128)S(1)}, u32[]{:S(2)}) copy-start(s32[13,13]{1,0:T(8,128)S(1)} %get-tuple-element.44) | copy-start | bytes 2032
  143.5 57.5 %copy-start.47 = (s32[1024]{0:T(1024)}, s32[1024]{0:T(1024)S(1)}, u32[]{:S(2)}) copy-start(s32[1024]{0:T(1024)S(1)} %broadcast_add_fusion) | copy-start | bytes 12292
  200.9 81.0 %copy-start.39 = (bf16[32,16]{1,0:T(8,128)(2,1)}, bf16[32,16]{1,0:T(8,128)(2,1)S(1)}, u32[]{:S(2)}) copy-start(bf16[32,16]{1,0:T(8,128)(2,1)S(1)} %reshape.558) | copy-start | bytes 3076
  201.4 125.0 %copy-start.43 = (f32[1024]{0:T(1024)}, f32[1024]{0:T(1024)S(1)}, u32[]{:S(2)}) copy-start(f32[1024]{0:T(1024)S(1)} %convert_element_type.437) | copy-start | bytes 12292
  333.3 36.5 %all-to-all-start.2 = ((bf16[8,80,1024]{2,1,0:T(8,128)(2,1)}), bf16[8,80,1024]{2,1,0:T(8,128)(2,1)}, u32[]{:S(2)}, u32[]{:S(2)}) async-start(bf16[8,80,1024]{2,1,0:T(8,128)(2,1)} %bitcast.174), calls=%async_computation.2 | async-start | bytes 2621440 | tf_op jit(solution)/shard_map/all_to_all | solution.py:231
  369.8 83.3 %all-to-all-start = ((bf16[8,80,1024]{2,1,0:T(8,128)(2,1)}), bf16[8,80,1024]{2,1,0:T(8,128)(2,1)S(1)}, u32[]{:S(2)}, u32[]{:S(2)}) async-start(bf16[8,80,1024]{2,1,0:T(8,128)(2,1)} %bitcast.173), calls=%async_computation | async-start | bytes 2621440 | tf_op jit(solution)/shard_map/all_to_all | solution.py:191
  453.2 67.7 %copy-start.22 = (bf16[8,80,1024]{2,1,0:T(8,128)(2,1)}, bf16[8,80,1024]{2,1,0:T(8,128)(2,1)S(1)}, u32[]{:S(2)}) copy-start(bf16[8,80,1024]{2,1,0:T(8,128)(2,1)S(1)} %all-to-all-done) | copy-start | bytes 3932164
  561.5 36.9 %all-to-all-start.1 = ((bf16[8,2,40960]{2,1,0:T(2,128)(2,1)}), bf16[8,2,40960]{2,1,0:T(2,128)(2,1)}, u32[]{:S(2)}, u32[]{:S(2)}) async-start(bf16[8,2,40960]{2,1,0:T(2,128)(2,1)} %reshape.633), calls=%async_computation.1 | async-start | bytes 2621440 | tf_op jit(solution)/shard_map/all_to_all | solution.py:199
  598.5 36.5 %all-to-all-start.3 = ((bf16[8,2,40960]{2,1,0:T(2,128)(2,1)}), bf16[8,2,40960]{2,1,0:T(2,128)(2,1)}, u32[]{:S(2)}, u32[]{:S(2)}) async-start(bf16[8,2,40960]{2,1,0:T(2,128)(2,1)} %reshape.635), calls=%async_computation.3 | async-start | bytes 2621440 | tf_op jit(solution)/shard_map/all_to_all | solution.py:246
  602.7 139.8 %all-gather.31.cloned.1.call-start = ((), (), s32[]{:S(2)}) async-start(), calls=%async_computation.19 | async-start | bytes 2621440 | tf_op jit(solution)/shard_map/all_gather | solution.py:317
  603.3 171.0 %all-gather.33.cloned.1.call-start = ((), (), s32[]{:S(2)}) async-start(), calls=%async_computation.20 | async-start | bytes 2621440 | tf_op jit(solution)/shard_map/all_gather | solution.py:318
  664.1 169.9 %reduce-scatter.19.cloned.1.call-start = ((), (), s32[]{:S(2)}) async-start(), calls=%async_computation.26 | async-start | bytes 540672
  688.7 304.1 %reduce-scatter.17.cloned.1.call-start = ((), (), s32[]{:S(2)}) async-start(), calls=%async_computation.25 | async-start | bytes 21626880 | tf_op jit(solution)/shard_map/reduce_scatter | solution.py:255
  703.0 434.0 %reduce-scatter.9.cloned.1.call-start = ((), (), s32[]{:S(2)}) async-start(), calls=%async_computation.21 | async-start | bytes 4325376 | tf_op jit(solution)/shard_map/reduce_scatter | solution.py:361
  719.6 559.7 %reduce-scatter.15.cloned.1.call-start = ((), (), s32[]{:S(2)}) async-start(), calls=%async_computation.24 | async-start | bytes 4325376 | tf_op jit(solution)/shard_map/reduce_scatter | solution.py:364
  722.5 699.0 %reduce-scatter.11.cloned.1.call-start = ((), (), s32[]{:S(2)}) async-start(), calls=%async_computation.22 | async-start | bytes 4325376 | tf_op jit(solution)/shard_map/reduce_scatter | solution.py:362
  786.8 777.2 %reduce-scatter.13.cloned.1.call-start = ((), (), s32[]{:S(2)}) async-start(), calls=%async_computation.23 | async-start | bytes 4325376 | tf_op jit(solution)/shard_map/reduce_scatter | solution.py:363
  (67 other events, 548.6 us)
Sparse Core Ops, SparseCore 0:
  10.9 59.1 all-gather.18
  72.9 55.2 all-gather.12
  131.1 55.4 all-gather.16
  188.3 34.2 all-gather.20
  224.2 35.4 all-gather.14
  262.5 56.3 all-gather.22
  320.8 64.6 all-gather.28
  387.3 65.7 all-gather.26
  455.0 65.7 all-gather.24
  605.1 35.5 all-gather.30
  664.3 33.0 all-gather.32
  700.0 133.9 reduce-scatter.18
  837.4 155.3 reduce-scatter.16
  995.5 141.4 reduce-scatter.8
  1139.7 139.5 reduce-scatter.14
  1282.0 139.3 reduce-scatter.10
  1424.1 139.7 reduce-scatter.12
where the time goes:
time: 1580 us; the launch traced here: 1570 us
  waiting for transfers between devices  936 us (59%)
  matrix products  226 us (14%)
  blocking collectives  163 us (10%)
  local copies, waits for them, and re-layouts  127 us (8%)
  other arithmetic  84.8 us (5%)
  starting transfers between devices  18.1 us (1%)
    reduce_scatter x1, waiting for transfers between devices, per_device(): lax.psum_scatter(value_term, ('expert', 'seq'), scatter_dimension=0, tile...  143 us
    reduce_scatter x1, waiting for transfers between devices, per_device(): lax.psum_scatter(output_term, ('expert', 'seq'), scatter_dimension=0, til...  142 us
    reduce_scatter x1, waiting for transfers between devices, per_device(): lax.psum_scatter(key_term, ('expert', 'seq'), scatter_dimension=0, tiled=...  142 us
    reduce_scatter x1, waiting for transfers between devices, per_device(): lax.psum_scatter(query_term, ('expert', 'seq'), scatter_dimension=0, tile...  137 us
    reduce_scatter x1, waiting for transfers between devices, per_device(): lax.psum_scatter(jnp.stack([jnp.einsum('rf,rd->fd', gate_backs, expert_in...  110 us
    unnamed x2, blocking collectives  80 us
    all_gather x1, blocking collectives, per_device(): lax.all_gather(router_weight, ('expert', 'seq'), axis=0, tiled=True)  67.3 us
    all_gather x1, waiting for transfers between devices, per_device(): gate_piece = lax.all_gather(gate_weight, 'seq', axis=1, tiled=True)  58.5 us
  transfers between devices with their start and end apart: 21, of which 14 were waited for; matrix products, arithmetic and copies ran while one was open for 25% of the time, Pallas kernels for 0%

commit v1 on v0

v1 whole, which is shorter than its diff:
```python
import math

import jax
import jax.numpy as jnp
from jax import lax
from jax.experimental import pallas as pl
from jax.experimental.pallas import tpu as pltpu
from jax.sharding import PartitionSpec as P

SPEC_0 = "qkb,bh->hqk"
SPEC_1 = "qhd,khd->hqk"
SPEC_2 = "hqk,khd->qhd"
SPEC_3 = "rd,fd->rf"
SPEC_4 = "rf,rd->fd"
SPEC_5 = "rd,re->de"
SPEC_6 = "re,de->rd"
SPEC_7 = "qkb,hqk->bh"
SPEC_8 = "hqk,qhd->khd"
MESH = pl.DeviceIdType.MESH
VMEM_LIMIT = 62 << 20
EXPERT, SEQ = "expert", "seq"
BOTH = (EXPERT, SEQ)

D = 1024
HEADS = 16
HDIM = 64
BUCKETS = 32
MAXDIST = 128


EPSILON = 1e-06
NEGATIVE = -1e30


def norm_factor(values):
    return lax.rsqrt(jnp.mean(values * values, axis=-1, keepdims=True) + EPSILON)


def gelu_tanh(values):
    return jax.nn.gelu(values, approximate=True)


def bucket_of(distance):
    exact_span = BUCKETS // 2
    above = jnp.zeros(distance.shape, jnp.int32)
    for number in range(exact_span):
        threshold = int(math.ceil(exact_span * (MAXDIST / exact_span) ** (number / exact_span)))
        above = above + (distance >= threshold).astype(jnp.int32)
    return jnp.where(distance < exact_span, distance, exact_span - 1 + above)


def tree_tables(lengths, parents):
    ordinal = jnp.arange(lengths.shape[0], dtype=jnp.int32)
    starts = jnp.cumsum(lengths) - lengths

    def chase(number, running):
        current, reaches = running
        current = jnp.sum(
            jnp.where(current[:, None] == ordinal[None, :], parents[None, :], 0), axis=1
        )
        reaches = jnp.maximum(reaches, (current[:, None] == ordinal[None, :]).astype(jnp.int32))
        return (current, reaches)

    begin = (ordinal, (ordinal[:, None] == ordinal[None, :]).astype(jnp.int32))
    unused, reaches = lax.fori_loop(0, lengths.shape[0], chase, begin)
    before = jnp.sum(reaches * lengths[None, :], axis=1) - lengths
    return (starts, before, reaches)


def token_info(token_rows, starts, before, reaches):
    ordinal = jnp.arange(starts.shape[0], dtype=jnp.int32)
    segment = jnp.sum((token_rows[:, None] >= starts[None, :]).astype(jnp.int32), axis=1) - 1
    member = segment[:, None] == ordinal[None, :]
    position = token_rows + jnp.sum(jnp.where(member, (before - starts)[None, :], 0), axis=1)
    lineage = jnp.sum(jnp.where(member[:, :, None], reaches[None, :, :], 0), axis=1)
    return (member.astype(jnp.float32), position, lineage.astype(jnp.float32))


def pair_terms(query_meta, key_meta, query_rows, key_rows, bias_grid):
    visible = jnp.dot(query_meta[2], key_meta[0].T, preferred_element_type=jnp.float32) > 0.5
    visible = visible & (key_rows[None, :] <= query_rows[:, None])
    distance = jnp.maximum(query_meta[1][:, None] - key_meta[1][None, :], 0)
    onehot = (
        bucket_of(distance)[:, :, None] == jnp.arange(BUCKETS, dtype=jnp.int32)[None, None, :]
    ).astype(jnp.bfloat16)
    pair_bias = jnp.einsum(SPEC_0, onehot, bias_grid, preferred_element_type=jnp.float32)
    return (visible, onehot, pair_bias)


def masked_scores(query_block, key_block, visible, pair_bias):
    scores = (
        jnp.einsum(SPEC_1, query_block, key_block, preferred_element_type=jnp.float32)
        * HDIM ** (-0.5)
        + pair_bias
    )
    return jnp.where(visible[None], scores, NEGATIVE)


def contract(left, right, dims):
    return lax.dot_general(left, right, (dims, ((), ())), preferred_element_type=jnp.float32)


def gelu_parts(values):
    root = 0.7978845608028654
    square = values * values
    swing = jnp.tanh(root * values * (1.0 + 0.044715 * square))
    half = 0.5 * (1.0 + swing)
    slope = half + 0.5 * values * (1.0 - swing * swing) * (root * (1.0 + 3 * 0.044715 * square))
    return values * half, slope


ORDER = (0, 1, 4, 5, 2, 3, 6, 7)


def expert_kernel(
    xs, gs, wg, wu, wd, ret_o, ret_b, dwg, dwu, dwd,
    xr, gr, act, gb, ub, po, pb, ro, rb, ro2, rb2, stage,
    in_send, in_recv, hop_send, hop_recv, rs_send, rs_recv, out_send, out_recv, stage_sem,
):
    e = lax.axis_index(EXPERT)
    s = lax.axis_index(SEQ)
    cap = xs.shape[0] // 8
    near_x, near_y = (e, s ^ 1), (e, s ^ 2)
    barrier = pltpu.get_barrier_semaphore()
    peers = [near_x, near_y] + [(e ^ d, s) for d in range(1, 8)]
    for peer in peers:
        pl.semaphore_signal(barrier, inc=1, device_id=peer, device_id_type=MESH)
    pl.semaphore_wait(barrier, len(peers))

    def remote(src, dst, send, recv, peer):
        return pltpu.make_async_remote_copy(
            src_ref=src, dst_ref=dst, send_sem=send, recv_sem=recv,
            device_id=peer, device_id_type=MESH,
        )

    def block(index):
        return pl.ds(pl.multiple_of(index * cap, 16), cap)

    tensors = ((xs, xr), (gs, gr))

    def entry(kind, place):
        src, dst = tensors[kind]
        d = ORDER[place]
        return remote(src.at[block(e ^ d)], dst.at[0, place], in_send.at[kind, place],
                      in_recv.at[kind, place], (e ^ d, s))

    def hop(kind, which, pair):
        buf = tensors[kind][1]
        two = pl.ds(2 * pair, 2)
        if which == 0:
            src, dst, peer = buf.at[0, two], buf.at[1, two], near_x
        elif which == 1:
            src, dst, peer = buf.at[0, two], buf.at[2, two], near_y
        elif kind == 0:
            src, dst, peer = buf.at[1, two], buf.at[3, two], near_y
        else:
            src, dst, peer = buf.at[2, two], buf.at[3, two], near_x
        return remote(src, dst, hop_send.at[kind, which, pair], hop_recv.at[kind, which, pair], peer)

    def rs(kind, which, c):
        part, one, two = ((po, ro, ro2), (pb, rb, rb2))[kind]
        first, second = ((near_x, near_y), (near_y, near_x))[kind]
        mine = 1 + kind
        if which == 0:
            src, dst, peer = part.at[mine, c], one.at[0, c], first
        elif which == 1:
            src, dst, peer = part.at[3, c], one.at[1, c], first
        else:
            src, dst, peer = part.at[2 - kind, c], two.at[c], second
        return remote(src, dst, rs_send.at[kind, which, c], rs_recv.at[kind, which, c], peer)

    def back(kind, place):
        part = (po, pb)[kind]
        ret = (ret_o, ret_b)[kind]
        c, i = place // 4, place % 4
        return remote(part.at[0, c, pl.ds(i * cap, cap)], ret.at[block(e)],
                      out_send.at[kind, place], out_recv.at[kind, place], (e ^ ORDER[place], s))

    def start_entries(c):
        for i in range(4):
            for kind in range(2):
                if ORDER[4 * c + i]:
                    entry(kind, 4 * c + i).start()

    def forward_pair(pair):
        for kind in range(2):
            for place in (2 * pair, 2 * pair + 1):
                if ORDER[place]:
                    entry(kind, place).wait_recv()
            hop(kind, 0, pair).start()
            hop(kind, 1, pair).start()

    def forward_corner(c):
        for pair in (2 * c, 2 * c + 1):
            hop(0, 0, pair).wait_recv()
            hop(0, 2, pair).start()
            hop(1, 1, pair).wait_recv()
            hop(1, 2, pair).start()

    def wait_hops(kind, which, c):
        for pair in (2 * c, 2 * c + 1):
            hop(kind, which, pair).wait_recv()

    def add_second(kind, c):
        rs(kind, 1, c).wait_recv()
        part, one = ((po, ro), (pb, rb))[kind]
        group = 2 - kind
        part[group, c] = (part[group, c].astype(jnp.float32) + one[1, c].astype(jnp.float32)).astype(jnp.bfloat16)
        rs(kind, 2, c).start()

    def finish(kind, c):
        rs(kind, 0, c).wait_recv()
        rs(kind, 2, c).wait_recv()
        part, one, two = ((po, ro, ro2), (pb, rb, rb2))[kind]
        part[0, c] = (
            part[0, c].astype(jnp.float32) + one[0, c].astype(jnp.float32) + two[c].astype(jnp.float32)
        ).astype(jnp.bfloat16)
        for i in range(4):
            if ORDER[4 * c + i]:
                back(kind, 4 * c + i).start()
            else:
                (ret_o, ret_b)[kind][block(e), :] = part[0, c, i * cap:(i + 1) * cap]

    start_entries(0)
    for src, dst in tensors:
        dst[0, 0] = src[block(e), :]
    forward_pair(0)
    forward_pair(1)
    start_entries(1)

    def unit(u, carry):
        q, c = lax.rem(u, 4), u // 4

        @pl.when(u == 1)
        def _():
            forward_corner(0)
            wait_hops(1, 0, 0)
            wait_hops(0, 1, 0)

        @pl.when(u == 3)
        def _():
            forward_pair(2)
            wait_hops(0, 2, 0)
            wait_hops(1, 2, 0)

        @pl.when(u == 4)
        def _():
            forward_pair(3)

        @pl.when(u == 5)
        def _():
            forward_corner(1)
            add_second(0, 0)
            add_second(1, 0)
            wait_hops(1, 0, 1)
            wait_hops(0, 1, 1)

        @pl.when(u == 7)
        def _():
            finish(0, 0)
            finish(1, 0)
            wait_hops(0, 2, 1)
            wait_hops(1, 2, 1)

        rows = 4 * cap
        x = xr[q, pl.ds(4 * c, 4)].reshape(rows, xs.shape[1])
        g = gr[q, pl.ds(4 * c, 4)].reshape(rows, xs.shape[1])
        gate = contract(x, wg[...], ((1,), (1,)))
        up = contract(x, wu[...], ((1,), (1,)))
        ag = contract(g, wd[...], ((1,), (1,)))
        value, slope = gelu_parts(gate)
        active = (value * up).astype(jnp.bfloat16)
        gate_back = (ag * up * slope).astype(jnp.bfloat16)
        up_back = (ag * value).astype(jnp.bfloat16)
        act[q, c] = active
        gb[q, c] = gate_back
        ub[q, c] = up_back
        po[q, c] = contract(active, wd[...], ((1,), (0,))).astype(jnp.bfloat16)
        pb[q, c] = (
            contract(gate_back, wg[...], ((1,), (0,))) + contract(up_back, wu[...], ((1,), (0,)))
        ).astype(jnp.bfloat16)

        for k, (kind, which) in ((1, (0, 0)), (2, (1, 0)), (3, (0, 1)), (3, (1, 1))):
            for half in range(2):
                @pl.when(u == k + 4 * half)
                def _():
                    rs(kind, which, half).start()
        return carry

    lax.fori_loop(0, 8, unit, 0)

    rows = 4 * cap

    def grads(left, right, dst):
        def part(u):
            q, c = lax.rem(u, 4), u // 4
            return contract(left[q, c], right[q, pl.ds(4 * c, 4)].reshape(rows, xs.shape[1]), ((0,), (0,)))

        def more(u, carry):
            stage[...] += part(u)
            return carry

        stage[...] = part(0)
        lax.fori_loop(1, 8, more, 0)
        done = pltpu.make_async_copy(stage, dst, stage_sem)
        done.start()
        return done

    gate_done = grads(gb, xr, dwg)
    add_second(0, 1)
    add_second(1, 1)
    gate_done.wait()
    up_done = grads(ub, xr, dwu)
    finish(0, 1)
    finish(1, 1)
    up_done.wait()
    grads(act, gr, dwd).wait()

    for kind in range(2):
        for place in range(8):
            if ORDER[place]:
                entry(kind, place).wait_send()
                back(kind, place).wait()
        for which in range(3):
            for pair in range(4):
                hop(kind, which, pair).wait_send()
            for c in range(2):
                rs(kind, which, c).wait_send()


def experts(send_rows, grad_rows, gate_weight, up_weight, down_weight):
    rows, width = send_rows.shape
    units = gate_weight.shape[0]
    cap = rows // 8
    low, full = jnp.bfloat16, jnp.float32
    vmem = pl.BlockSpec(memory_space=pltpu.VMEM)
    hbm = pl.BlockSpec(memory_space=pl.ANY)
    dma = pltpu.SemaphoreType.DMA
    return pl.pallas_call(
        expert_kernel,
        out_shape=(
            jax.ShapeDtypeStruct((rows, width), low),
            jax.ShapeDtypeStruct((rows, width), low),
        ) + (jax.ShapeDtypeStruct((units, width), full),) * 3,
        in_specs=[vmem] * 5,
        out_specs=(vmem, vmem, hbm, hbm, hbm),
        scratch_shapes=[
            pltpu.VMEM((4, 8, cap, width), low),
            pltpu.VMEM((4, 8, cap, width), low),
            pltpu.VMEM((4, 2, 4 * cap, units), low),
            pltpu.VMEM((4, 2, 4 * cap, units), low),
            pltpu.VMEM((4, 2, 4 * cap, units), low),
            pltpu.VMEM((4, 2, 4 * cap, width), low),
            pltpu.VMEM((4, 2, 4 * cap, width), low),
            pltpu.VMEM((2, 2, 4 * cap, width), low),
            pltpu.VMEM((2, 2, 4 * cap, width), low),
            pltpu.VMEM((2, 4 * cap, width), low),
            pltpu.VMEM((2, 4 * cap, width), low),
            pltpu.VMEM((units, width), full),
            dma((2, 8)), dma((2, 8)),
            dma((2, 3, 4)), dma((2, 3, 4)),
            dma((2, 3, 2)), dma((2, 3, 2)),
            dma((2, 8)), dma((2, 8)),
            dma,
        ],
        compiler_params=pltpu.CompilerParams(
            collective_id=1, has_side_effects=True, vmem_limit_bytes=VMEM_LIMIT
        ),
        cost_estimate=pl.CostEstimate(flops=2 * 9 * 4 * rows * units * width, bytes_accessed=20 << 20, transcendentals=4 * rows * units),
        name="experts",
    )(send_rows, grad_rows, gate_weight, up_weight, down_weight)


def remote(src, dst, send, recv, peer):
    return pltpu.make_async_remote_copy(
        src_ref=src, dst_ref=dst, send_sem=send, recv_sem=recv,
        device_id=peer, device_id_type=MESH,
    )


def greet(peers):
    barrier = pltpu.get_barrier_semaphore()
    for peer in peers:
        pl.semaphore_signal(barrier, inc=1, device_id=peer, device_id_type=MESH)
    pl.semaphore_wait(barrier, len(peers))


def aligned(index, size):
    return pl.ds(pl.multiple_of(index * size, size), size)


ZHOPS = (2, 4, 6)


def project_kernel(
    tokens, wq, wk, wv, misc, all_tokens, qkv, cols, params,
    part, tags, tag_sum, all_tags,
    t_send, t_recv, w_send, w_recv, m_send, m_recv, c_send, c_recv, n_send, n_recv,
):
    e, s = lax.axis_index(EXPERT), lax.axis_index(SEQ)
    near_x, near_y, corner = (e, s ^ 1), (e, s ^ 2), (e, s ^ 3)
    around = (near_x, near_y, corner)
    along = [(e ^ d, s) for d in (1,) + ZHOPS]
    greet(list(around) + along)
    rows, width = tokens.shape
    slim = wq.shape[0]
    shard = width // 4
    weights = (wq, wk, wv)

    def send_tokens(k):
        return remote(tokens, all_tokens.at[aligned(s, rows)], t_send.at[k], t_recv.at[k], around[k])

    def pass_tokens(k):
        piece = pl.ds(pl.multiple_of((s ^ (1 + k)) * rows + k * (rows // 2), rows // 2), rows // 2)
        view = all_tokens.at[piece]
        return remote(view, view, t_send.at[2 + k], t_recv.at[2 + k], around[1 - k])

    def send_cols(k, m):
        return remote(
            weights[m].at[:, aligned(s ^ (k + 1), shard)], part.at[m, aligned(s, slim)],
            w_send.at[k, m], w_recv.at[k, m], around[k],
        )

    def send_tags(k):
        return remote(misc, tags.at[k], m_send.at[k], m_recv.at[k], around[k])

    hops = (1,) + ZHOPS

    def share(k):
        return remote(part, cols.at[:, aligned(e, 4 * slim)], c_send.at[k], c_recv.at[k], (e ^ hops[k], s))

    def share_tags(k):
        return remote(tag_sum, all_tags.at[k], n_send.at[k], n_recv.at[k], (e ^ hops[k], s))

    def relay(k):
        view = cols.at[:, aligned(e ^ hops[k], 4 * slim)]
        return remote(view, view, c_send.at[3 + k], c_recv.at[3 + k], (e ^ 1, s))

    def relay_tags(k):
        return remote(all_tags.at[k], all_tags.at[3 + k], n_send.at[3 + k], n_recv.at[3 + k], (e ^ 1, s))

    for k in range(3):
        for m in range(3):
            send_cols(k, m).start()
        send_tags(k).start()
    for k in range(2):
        send_tokens(k).start()
    for m in range(3):
        part[m, aligned(s, slim), :] = weights[m][:, aligned(s, shard)]
    all_tokens[aligned(s, rows), :] = tokens[...]
    total = misc[...].astype(jnp.float32)
    for k in range(3):
        send_tags(k).wait_recv()
        total += tags[k].astype(jnp.float32)
    tag_sum[...] = total.astype(jnp.bfloat16)
    for k in range(3):
        for m in range(3):
            send_cols(k, m).wait_recv()
    for k in range(4):
        share_tags(k).start()
        share(k).start()
    cols[:, aligned(e, 4 * slim), :] = part[...]
    for k in range(2):
        send_tokens(k).wait_recv()
        pass_tokens(k).start()
    for k in range(1, 4):
        share_tags(k).wait_recv()
        relay_tags(k).start()
        share(k).wait_recv()
        relay(k).start()
    share_tags(0).wait_recv()
    share(0).wait_recv()
    for k in range(1, 4):
        relay_tags(k).wait_recv()
        relay(k).wait_recv()
    for k in range(7):
        total += all_tags[k].astype(jnp.float32)
    params[...] = total
    gain = total[0:1]

    def group(q, carry):
        @pl.when(q == 3)
        def _():
            for k in range(2):
                pass_tokens(k).wait_recv()
        place = aligned(s ^ q, rows)
        values = all_tokens[place, :].astype(jnp.float32)
        normed = (values * norm_factor(values) * gain).astype(jnp.bfloat16)
        for m in range(3):
            out = contract(normed, cols[m], ((1,), (0,)))
            if m == 0:
                out = out.astype(jnp.bfloat16).astype(jnp.float32) * HDIM ** (-0.5)
            qkv[place, m * shard:(m + 1) * shard] = out.astype(jnp.bfloat16)
        return carry

    lax.fori_loop(0, 4, group, 0)
    for k in range(2):
        send_tokens(k).wait_send()
        pass_tokens(k).wait_send()
    for k in range(3):
        for m in range(3):
            send_cols(k, m).wait_send()
        send_tags(k).wait_send()
    for k in range(4):
        share(k).wait_send()
        share_tags(k).wait_send()
    for k in range(1, 4):
        relay(k).wait_send()
        relay_tags(k).wait_send()


def project(tokens, wq, wk, wv, misc):
    rows, width = tokens.shape
    slim, shard = wq.shape[0], width // 4
    low, full = jnp.bfloat16, jnp.float32
    vmem = pl.BlockSpec(memory_space=pltpu.VMEM)
    dma = pltpu.SemaphoreType.DMA
    return pl.pallas_call(
        project_kernel,
        out_shape=(
            jax.ShapeDtypeStruct((4 * rows, width), low),
            jax.ShapeDtypeStruct((4 * rows, 3 * shard), low),
            jax.ShapeDtypeStruct((3, width, shard), low),
            jax.ShapeDtypeStruct(misc.shape, full),
        ),
        in_specs=[vmem] * 5,
        out_specs=(vmem,) * 4,
        scratch_shapes=[
            pltpu.VMEM((3, 4 * slim, shard), low),
            pltpu.VMEM((3,) + misc.shape, low),
            pltpu.VMEM(misc.shape, low),
            pltpu.VMEM((7,) + misc.shape, low),
            dma((4,)), dma((4,)), dma((3, 3)), dma((3, 3)), dma((3,)), dma((3,)),
            dma((7,)), dma((7,)), dma((7,)), dma((7,)),
        ],
        compiler_params=pltpu.CompilerParams(
            collective_id=2, has_side_effects=True, vmem_limit_bytes=VMEM_LIMIT
        ),
        cost_estimate=pl.CostEstimate(flops=24 * rows * width * shard, bytes_accessed=10 << 20, transcendentals=0),
        name="project",
    )(tokens, wq, wk, wv, misc)


def segment_scalars(lengths, parents, before_mem, reach_mem):
    count = lengths.shape[1]
    start = jnp.int32(0)
    found = []
    for k in range(count):
        length = lengths[0, k]
        if k == 0:
            before, reach = jnp.int32(0), jnp.int32(1)
        else:
            parent = parents[0, k]
            before = before_mem[parent] + lengths[0, parent]
            reach = reach_mem[parent] | (1 << k)
        before_mem[k] = before
        reach_mem[k] = reach
        found.append((start, before, reach, length))
        start = start + length
    return found


def token_columns(found, ids):
    offset = jnp.zeros(ids.shape, jnp.int32)
    reach = jnp.full(ids.shape, 1, jnp.int32)
    own = jnp.full(ids.shape, 1, jnp.int32)
    for k, (start, before, bits, _) in enumerate(found):
        if k:
            after = ids >= start
            offset = jnp.where(after, before - start, offset)
            reach = jnp.where(after, bits, reach)
            own = jnp.where(after, 1 << k, own)
    return ids + offset, reach, own


LAST = 127


def bias_tables(params, s):
    flat = params[2:3, 0:BUCKETS * HEADS]
    lane = lax.broadcasted_iota(jnp.int32, (8, BUCKETS * HEADS), 1)
    head = lax.broadcasted_iota(jnp.int32, (8, BUCKETS * HEADS), 0)
    heads_here = HEADS // 4
    chosen = jnp.where((lane % HEADS) == s * heads_here + head, jnp.broadcast_to(flat, lane.shape), 0.0)
    entry = lax.broadcasted_iota(jnp.int32, (BUCKETS * HEADS, LAST + 1), 0) // HEADS
    distance = lax.broadcasted_iota(jnp.int32, (BUCKETS * HEADS, LAST + 1), 1)
    hot = jnp.where(entry == bucket_of(distance), 1.0, 0.0)
    table = contract(chosen.astype(jnp.bfloat16), hot.astype(jnp.bfloat16), ((1,), (0,)))
    spot = lax.broadcasted_iota(jnp.int32, table.shape, 1)
    return jnp.where(spot == LAST, NEGATIVE, table)


def pair_index(found, first, rows, count):
    ids = first + lax.broadcasted_iota(jnp.int32, (rows, 1), 0)
    keys = lax.broadcasted_iota(jnp.int32, (1, count), 1)
    place, reach, _ = token_columns(found, ids)
    key_place, _, key_own = token_columns(found, keys)
    seen = ((reach & key_own) != 0) & (keys <= ids)
    return jnp.where(seen, jnp.minimum(place - key_place, LAST - 1), LAST), place, reach


def looked_up(row, index):
    rows, count = index.shape
    table = jnp.broadcast_to(row, (rows, LAST + 1))
    pieces = [
        jnp.take_along_axis(table, index[:, k * 128:(k + 1) * 128], axis=1)
        for k in range(count // 128)
    ]
    return jnp.concatenate(pieces, axis=1)


def attend_kernel(lengths, parents, qkv, params, out, index, table, before_mem, reach_mem):
    s = lax.axis_index(SEQ)
    found = segment_scalars(lengths, parents, before_mem, reach_mem)
    table[...] = bias_tables(params, s)
    total = qkv.shape[0]
    block = 256
    shard = qkv.shape[1] // 3
    for r in range(total // block):
        count = (r + 1) * block
        index[:, :count] = pair_index(found, r * block, block, count)[0]

        def pair(h, carry):
            place = aligned(h, 128)
            q = qkv[r * block:count, place]
            k = qkv[0:count, aligned(h + shard // 128, 128)]
            v = qkv[0:count, aligned(h + 2 * shard // 128, 128)]
            lane = lax.broadcasted_iota(jnp.int32, (block, 128), 1)
            results = []
            for side in range(2):
                mine = (lane // HDIM) == side
                scores = contract(jnp.where(mine, q, jnp.zeros_like(q)), k, ((1,), (1,)))
                scores = scores + looked_up(table[pl.ds(2 * h + side, 1), :], index[:, :count])
                expo = jnp.exp(scores - jnp.max(scores, axis=1, keepdims=True))
                probs = (expo / jnp.sum(expo, axis=1, keepdims=True)).astype(jnp.bfloat16)
                results.append(contract(probs, v, ((1,), (0,))))
            out[r * block:count, place] = jnp.where((lane // HDIM) == 0, results[0], results[1]).astype(jnp.bfloat16)
            return carry

        lax.fori_loop(0, shard // 128, pair, 0)


def attend(lengths, parents, qkv, params):
    total, shard = qkv.shape[0], qkv.shape[1] // 3
    vmem, smem = pl.BlockSpec(memory_space=pltpu.VMEM), pl.BlockSpec(memory_space=pltpu.SMEM)
    return pl.pallas_call(
        attend_kernel,
        out_shape=jax.ShapeDtypeStruct((total, shard), jnp.bfloat16),
        in_specs=[smem, smem, vmem, vmem],
        out_specs=vmem,
        scratch_shapes=[
            pltpu.VMEM((256, total), jnp.int32), pltpu.VMEM((8, 128), jnp.float32),
            pltpu.SMEM((16,), jnp.int32), pltpu.SMEM((16,), jnp.int32),
        ],
        compiler_params=pltpu.CompilerParams(vmem_limit_bytes=VMEM_LIMIT),
        cost_estimate=pl.CostEstimate(flops=4 * total * total * shard, bytes_accessed=4 << 20, transcendentals=2 * total * total),
        name="attend",
    )(lengths, parents, qkv, params)


def attend_back_kernel(lengths, parents, qkv, params, grad, dqkv, bias_grad,
                       index, spots, table, near, dk, dv, before_mem, reach_mem):
    s = lax.axis_index(SEQ)
    found = segment_scalars(lengths, parents, before_mem, reach_mem)
    table[...] = bias_tables(params, s)
    total = qkv.shape[0]
    block = 256
    shard = qkv.shape[1] // 3
    dk[...] = jnp.zeros_like(dk)
    dv[...] = jnp.zeros_like(dv)
    near[...] = jnp.zeros_like(near)
    for r in range(total // block):
        count = (r + 1) * block
        here, place, reach = pair_index(found, r * block, block, count)
        index[:, :count] = here
        step = lax.broadcasted_iota(jnp.int32, (block, 128), 1)
        wanted = place - step
        spot = jnp.full((block, 128), -1, jnp.int32)
        for k, (start, before, _, length) in enumerate(found):
            inside = ((reach & (1 << k)) != 0) & (wanted >= before) & (wanted < before + length)
            spot = jnp.where(inside, wanted + (start - before), spot)
        spots[...] = jnp.where(step == LAST, -1, spot)

        def pair(h, carry):
            lanes = aligned(h, 128)
            q = qkv[r * block:count, lanes]
            k = qkv[0:count, aligned(h + shard // 128, 128)]
            v = qkv[0:count, aligned(h + 2 * shard // 128, 128)]
            g = grad[r * block:count, lanes]
            lane = lax.broadcasted_iota(jnp.int32, (block, 128), 1)
            dq = None
            key_sum, value_sum = 0.0, 0.0
            for side in range(2):
                mine = (lane // HDIM) == side
                q_side = jnp.where(mine, q, jnp.zeros_like(q))
                g_side = jnp.where(mine, g, jnp.zeros_like(g))
                scores = contract(q_side, k, ((1,), (1,)))
                scores = scores + looked_up(table[pl.ds(2 * h + side, 1), :], index[:, :count])
                expo = jnp.exp(scores - jnp.max(scores, axis=1, keepdims=True))
                soft = expo / jnp.sum(expo, axis=1, keepdims=True)
                dprob = contract(g_side, v, ((1,), (1,)))
                delta = jnp.sum(soft * dprob, axis=1, keepdims=True)
                score_grad = (soft * (dprob - delta)).astype(jnp.bfloat16)
                wide = score_grad.astype(jnp.float32)
                part = contract(score_grad, k, ((1,), (0,)))
                dq = part if side == 0 else jnp.where(mine, part, dq)
                key_sum = key_sum + contract(score_grad, q_side, ((0,), (0,)))
                value_sum = value_sum + contract(soft.astype(jnp.bfloat16), g_side, ((0,), (0,)))
                close = jnp.zeros((block, 128), jnp.float32)
                everything = jnp.zeros((block, 128), jnp.float32)
                for b in range(count // 128):
                    piece = wide[:, b * 128:(b + 1) * 128]
                    local = spots[...] - b * 128
                    there = (local >= 0) & (local < 128)
                    taken = jnp.take_along_axis(piece, jnp.where(there, local, 0), axis=1)
                    close = close + jnp.where(there, taken, 0.0)
                    everything = everything + piece
                for kind, values in enumerate((close, everything)):
                    near[kind, 2 * h + side] += jnp.sum(values.reshape(block // 8, 8, 128), axis=0)
            dqkv[r * block:count, lanes] = (dq * HDIM ** (-0.5)).astype(jnp.bfloat16)
            dk[0:count, lanes] += key_sum
            dv[0:count, lanes] += value_sum
            return carry

        lax.fori_loop(0, shard // 128, pair, 0)
    dqkv[:, shard:2 * shard] = dk[...].astype(jnp.bfloat16)
    dqkv[:, 2 * shard:3 * shard] = dv[...].astype(jnp.bfloat16)
    close, everything = (
        jnp.concatenate([jnp.sum(near[kind, h], axis=0, keepdims=True) for h in range(8)], axis=0) for kind in range(2)
    )
    far = jnp.sum(everything, axis=1, keepdims=True) - jnp.sum(close, axis=1, keepdims=True)
    spot = lax.broadcasted_iota(jnp.int32, close.shape, 1)
    by_distance = jnp.where(spot == LAST, far, close)
    lane = lax.broadcasted_iota(jnp.int32, (128, BUCKETS * HEADS), 1)
    distance = lax.broadcasted_iota(jnp.int32, (128, BUCKETS * HEADS), 0)
    hot = jnp.where((lane // HEADS) == bucket_of(distance), 1.0, 0.0)
    spread = lax.dot_general(by_distance, hot, (((1,), (0,)), ((), ())),
                             precision=lax.Precision.HIGHEST, preferred_element_type=jnp.float32)
    head = lax.broadcasted_iota(jnp.int32, spread.shape, 0)
    lane = lax.broadcasted_iota(jnp.int32, spread.shape, 1)
    here = ((lane % HEADS) == s * (HEADS // 4) + head) & (head < HEADS // 4)
    bias_grad[...] = jnp.broadcast_to(jnp.sum(jnp.where(here, spread, 0.0), axis=0, keepdims=True), bias_grad.shape)


def attend_back(lengths, parents, qkv, params, grad):
    total, shard = qkv.shape[0], qkv.shape[1] // 3
    full = jnp.float32
    vmem, smem = pl.BlockSpec(memory_space=pltpu.VMEM), pl.BlockSpec(memory_space=pltpu.SMEM)
    return pl.pallas_call(
        attend_back_kernel,
        out_shape=(
            jax.ShapeDtypeStruct((total, 3 * shard), jnp.bfloat16),
            jax.ShapeDtypeStruct((8, BUCKETS * HEADS), full),
        ),
        in_specs=[smem, smem, vmem, vmem, vmem],
        out_specs=(vmem, vmem),
        scratch_shapes=[
            pltpu.VMEM((256, total), jnp.int32), pltpu.VMEM((256, 128), jnp.int32),
            pltpu.VMEM((8, 128), full), pltpu.VMEM((2, 8, 8, 128), full),
            pltpu.VMEM((total, shard), full), pltpu.VMEM((total, shard), full),
            pltpu.SMEM((16,), jnp.int32), pltpu.SMEM((16,), jnp.int32),
        ],
        compiler_params=pltpu.CompilerParams(vmem_limit_bytes=VMEM_LIMIT),
        cost_estimate=pl.CostEstimate(flops=10 * total * total * shard, bytes_accessed=6 << 20, transcendentals=2 * total * total),
        name="attend_back",
    )(lengths, parents, qkv, params, grad)


def routing(residual, params, ids, ids_row, cap):
    rows = residual.shape[0]
    full = jnp.float32
    scale = norm_factor(residual)
    unit = residual * scale
    normed = (unit * params[1:2]).astype(jnp.bfloat16)
    router = params[8:16]
    logits = contract(normed, router.astype(jnp.bfloat16), ((1,), (1,)))
    expo = jnp.exp(logits - jnp.max(logits, axis=1, keepdims=True))
    prob = expo / jnp.sum(expo, axis=1, keepdims=True)
    lane = lax.broadcasted_iota(jnp.int32, (rows, 8), 1)
    hot = [jnp.where(ids[:, k:k + 1] == lane, 1.0, 0.0).astype(full) for k in range(2)]
    chosen = [jnp.sum(h * prob, axis=1, keepdims=True) for h in hot]
    chosen_sum = chosen[0] + chosen[1]
    shares = [c / chosen_sum for c in chosen]
    down = lax.broadcasted_iota(jnp.int32, (rows, rows), 0)
    across = lax.broadcasted_iota(jnp.int32, (rows, rows), 1)
    before = jnp.where(across < down, 1.0, 0.0).astype(jnp.bfloat16)
    earlier = contract(before, (hot[0] + hot[1]).astype(jnp.bfloat16), ((1,), (0,)))
    slots = [jnp.sum(h * earlier, axis=1, keepdims=True) for h in hot]
    kept = [jnp.where(slot < cap, 1.0, 0.0) for slot in slots]
    target = [
        jnp.where(slots[k] < cap, ids[:, k:k + 1] * cap + slots[k].astype(jnp.int32), -1) for k in range(2)
    ]
    level = lax.broadcasted_iota(jnp.int32, (8, rows), 0)
    hot_row = [jnp.where(ids_row[k:k + 1] == level, 1.0, 0.0).astype(full) for k in range(2)]
    after = jnp.where(down < across, 1.0, 0.0).astype(jnp.bfloat16)
    earlier_row = contract((hot_row[0] + hot_row[1]).astype(jnp.bfloat16), after, ((1,), (0,)))
    slot_row = [jnp.sum(h * earlier_row, axis=0, keepdims=True) for h in hot_row]
    target_row = [
        jnp.where(slot_row[k] < cap, ids_row[k:k + 1] * cap + slot_row[k].astype(jnp.int32), -1) for k in range(2)
    ]
    return scale, unit, normed, router, prob, hot, chosen_sum, shares, kept, target, target_row


def dispatch_kernel(att, wo, tokens, cotangent, params, ids, ids_row, xs, gs, residual, landed, send, recv):
    e, s = lax.axis_index(EXPERT), lax.axis_index(SEQ)
    around = [(e, s ^ k) for k in range(1, 4)]
    greet(around)
    rows, width = tokens.shape
    shard = att.shape[1]
    cap = xs.shape[0] // 8

    def give(k):
        return remote(att.at[aligned(s ^ (k + 1), rows)], landed.at[s], send.at[k], recv.at[k], around[k])

    for k in (2, 0, 1):
        give(k).start()
    landed[s] = att[aligned(s, rows), :]
    total = tokens[...].astype(jnp.float32)
    total += contract(landed[s], wo[aligned(s, shard), :], ((1,), (0,)))
    for k in range(3):
        give(k).wait_recv()
        total += contract(landed[s ^ (k + 1)], wo[aligned(s ^ (k + 1), shard), :], ((1,), (0,)))
    residual[...] = total
    _, _, normed, _, _, _, _, shares, kept, _, target_row = routing(total, params[...], ids[...], ids_row[...], cap)
    place = lax.broadcasted_iota(jnp.int32, (8 * cap, rows), 0)
    hot = [jnp.where(place == target_row[k], 1.0, 0.0).astype(jnp.bfloat16) for k in range(2)]
    xs[...] = contract(hot[0] + hot[1], normed, ((1,), (0,))).astype(jnp.bfloat16)
    grad = cotangent[...].astype(jnp.float32)
    weighted = [((shares[k] * kept[k]) * grad).astype(jnp.bfloat16) for k in range(2)]
    gs[...] = (
        contract(hot[0], weighted[0], ((1,), (0,))) + contract(hot[1], weighted[1], ((1,), (0,)))
    ).astype(jnp.bfloat16)
    for k in range(3):
        give(k).wait_send()


def dispatch(att, wo, tokens, cotangent, params, ids, ids_row):
    rows, width = tokens.shape
    cap = 10 * rows // 32
    low, full = jnp.bfloat16, jnp.float32
    vmem = pl.BlockSpec(memory_space=pltpu.VMEM)
    dma = pltpu.SemaphoreType.DMA
    return pl.pallas_call(
        dispatch_kernel,
        out_shape=(
            jax.ShapeDtypeStruct((8 * cap, width), low),
            jax.ShapeDtypeStruct((8 * cap, width), low),
            jax.ShapeDtypeStruct((rows, width), full),
        ),
        in_specs=[vmem] * 7,
        out_specs=(vmem,) * 3,
        scratch_shapes=[pltpu.VMEM((4, rows, att.shape[1]), low), dma((3,)), dma((3,))],
        compiler_params=pltpu.CompilerParams(
            collective_id=3, has_side_effects=True, vmem_limit_bytes=VMEM_LIMIT
        ),
        cost_estimate=pl.CostEstimate(flops=6 * rows * width * width, bytes_accessed=8 << 20, transcendentals=rows * 8),
        name="dispatch",
    )(att, wo, tokens, cotangent, params, ids, ids_row)


def combine_kernel(ret_o, ret_b, residual, cotangent, wo, params, ids, ids_row,
                   layer_out, residual_grad, datt, aog_cols, small,
                   datt_own, aog_own, send, recv):
    e, s = lax.axis_index(EXPERT), lax.axis_index(SEQ)
    around = [(e, s ^ k) for k in range(1, 4)]
    greet(around)
    rows, width = residual.shape
    shard = datt.shape[1]
    cap = ret_o.shape[0] // 8
    full = jnp.float32
    high = lax.Precision.HIGHEST
    held = residual[...]
    scale, unit, normed, router, prob, hot, chosen_sum, shares, kept, target, _ = routing(
        held, params[...], ids[...], ids_row[...], cap
    )
    place = lax.broadcasted_iota(jnp.int32, (rows, 8 * cap), 1)
    pick = [jnp.where(place == target[k], 1.0, 0.0).astype(jnp.bfloat16) for k in range(2)]
    grad = cotangent[...].astype(full)
    mixture = jnp.zeros((rows, width), full)
    share_grad = []
    for k in range(2):
        picked = contract(pick[k], ret_o[...], ((1,), (0,)))
        mixture += (shares[k] * kept[k]) * picked
        share_grad.append(jnp.sum(grad * picked, axis=1, keepdims=True) * kept[k])
    layer_out[...] = (held + mixture).astype(jnp.bfloat16)
    inner = shares[0] * share_grad[0] + shares[1] * share_grad[1]
    prob_grad = sum(hot[k] * ((share_grad[k] - inner) / chosen_sum) for k in range(2))
    logit_grad = prob * (prob_grad - jnp.sum(prob * prob_grad, axis=1, keepdims=True))
    router_term = lax.dot_general(logit_grad, normed.astype(full), (((0,), (0,)), ((), ())),
                                  precision=high, preferred_element_type=full)
    normed_grad = contract(pick[0] + pick[1], ret_b[...], ((1,), (0,))) + lax.dot_general(
        logit_grad, router, (((1,), (0,)), ((), ())), precision=high, preferred_element_type=full
    )
    gain_term = jnp.sum(normed_grad * unit, axis=0, keepdims=True)
    unit_grad = normed_grad * params[1:2]
    back = grad + scale * (unit_grad - unit * jnp.mean(unit_grad * unit, axis=1, keepdims=True))
    residual_grad[...] = back
    rounded = back.astype(jnp.bfloat16)
    aog_own[...] = rounded
    datt_own[...] = contract(rounded, wo[...], ((1,), (1,))).astype(jnp.bfloat16)

    def give(kind, k):
        src, dst = ((datt_own, datt), (aog_own, aog_cols))[kind]
        return remote(src.at[:, aligned(s ^ (k + 1), shard)], dst.at[aligned(s, rows)],
                      send.at[kind, k], recv.at[kind, k], around[k])

    for kind in range(2):
        for k in (2, 0, 1):
            give(kind, k).start()
    datt[aligned(s, rows), :] = datt_own[:, aligned(s, shard)]
    aog_cols[aligned(s, rows), :] = aog_own[:, aligned(s, shard)]
    lane = lax.broadcasted_iota(jnp.int32, (1, width), 1)
    sums = jnp.where(lane == 0, jnp.sum(held * held), jnp.where(lane == 1, jnp.sum(mixture * mixture), 0.0))
    small[0:8, :] = jnp.zeros((8, width), full)
    small[1:2, :] = gain_term
    small[3:4, :] = sums
    small[8:16, :] = router_term
    for kind in range(2):
        for k in range(3):
            give(kind, k).wait()


def combine(ret_o, ret_b, residual, cotangent, wo, params, ids, ids_row):
    rows, width = residual.shape
    shard = width // 4
    low, full = jnp.bfloat16, jnp.float32
    vmem = pl.BlockSpec(memory_space=pltpu.VMEM)
    dma = pltpu.SemaphoreType.DMA
    return pl.pallas_call(
        combine_kernel,
        out_shape=(
            jax.ShapeDtypeStruct((rows, width), low),
            jax.ShapeDtypeStruct((rows, width), full),
            jax.ShapeDtypeStruct((4 * rows, shard), low),
            jax.ShapeDtypeStruct((4 * rows, shard), low),
            jax.ShapeDtypeStruct((16, width), full),
        ),
        in_specs=[vmem] * 8,
        out_specs=(vmem,) * 5,
        scratch_shapes=[pltpu.VMEM((rows, width), low), pltpu.VMEM((rows, width), low), dma((2, 3)), dma((2, 3))],
        compiler_params=pltpu.CompilerParams(
            collective_id=4, has_side_effects=True, vmem_limit_bytes=VMEM_LIMIT
        ),
        cost_estimate=pl.CostEstimate(flops=6 * rows * width * width, bytes_accessed=12 << 20, transcendentals=rows * 8),
        name="combine",
    )(ret_o, ret_b, residual, cotangent, wo, params, ids, ids_row)


def finish_kernel(
    all_tokens, dqkv, cols, att_full, aog_cols, residual_grad, params, small, bias_grad,
    tokens_grad, dwq, dwk, dwv, dwo, small_sum,
    halves, core_got, sums, z_got, final, parts, first_got, second_got, mine, normed, tally, tally_got,
    core_send, core_recv, z_send, z_recv, a_send, a_recv, n_send, n_recv, m_send, m_recv,
):
    e, s = lax.axis_index(EXPERT), lax.axis_index(SEQ)
    z, c = e // 2, lax.rem(e, 2)
    near_x, near_y = (e, s ^ 1), (e, s ^ 2)
    around = [(e, s ^ k) for k in range(1, 4)]
    hops = (1,) + ZHOPS
    greet(around + [(e ^ d, s) for d in hops])
    full, low = jnp.float32, jnp.bfloat16
    rows, width = residual_grad.shape
    shard = cols.shape[2]
    slim = dwq.shape[0]
    outs = (dwo, dwv, dwk, dwq)
    gain = params[0:1]

    def units(q):
        values = all_tokens[aligned(s ^ q, rows), :].astype(full)
        scale = norm_factor(values)
        return values * scale, scale

    def core_copy(m):
        return remote(halves.at[1 - c, m], core_got.at[m], core_send.at[m], core_recv.at[m], (e ^ 1, s))

    def z_copy(m, k):
        return remote(sums.at[m, z ^ k], z_got.at[k - 1, m], z_send.at[m, k - 1], z_recv.at[m, k - 1], (e ^ (2 * k), s))

    def a_copy(m, k):
        return remote(final.at[m, aligned(s ^ (k + 1), slim)], outs[m].at[:, aligned(s, shard)],
                      a_send.at[m, k], a_recv.at[m, k], around[k])

    def n_copy(kind, which):
        first, second = ((near_x, near_y), (near_y, near_x))[kind]
        if which < 2:
            src = parts.at[(1 + kind, 3)[which], kind]
            return remote(src, first_got.at[kind, which], n_send.at[kind, which], n_recv.at[kind, which], first)
        return remote(parts.at[2 - kind, kind], second_got.at[kind], n_send.at[kind, 2], n_recv.at[kind, 2], second)

    def store_halves(m, zone, block):
        for half in range(2):
            halves[half, m, zone] = block[half * (shard // 2):(half + 1) * (shard // 2)].astype(low)

    def norm_block(q, carry):
        unit, _ = units(q)
        normed[aligned(s ^ q, rows), :] = (unit * gain).astype(low)
        return carry

    def output_zone(j, carry):
        store_halves(0, j, contract(att_full[:, aligned(j, shard)], aog_cols[...], ((0,), (0,))))
        return carry

    lax.fori_loop(0, 4, output_zone, 0)
    core_copy(0).start()
    lax.fori_loop(0, 4, norm_block, 0)

    def qkv_zone(j, carry):
        block = contract(normed[:, aligned(j, shard)], dqkv[...], ((0,), (0,)))
        for m in range(3):
            store_halves(3 - m, j, block[:, m * shard:(m + 1) * shard])
        return carry

    lax.fori_loop(0, 4, qkv_zone, 0)
    for m in range(1, 4):
        core_copy(m).start()

    def add_core(m):
        core_copy(m).wait_recv()
        for j in range(4):
            sums[m, j] = (halves[c, m, j].astype(full) + core_got[m, j].astype(full)).astype(low)
        for k in range(1, 4):
            z_copy(m, k).start()

    add_core(0)
    tally[0] = small[...]
    tally[0, 0:1] = jnp.zeros((1, width), full)
    tally[0, 2:3, 0:BUCKETS * HEADS] = bias_grad[0:1]

    def back_block(i, carry):
        q = 3 - i
        place = aligned(s ^ q, rows)
        d = dqkv[place, :]
        total = jnp.zeros((rows, width), full)
        for m in range(3):
            total += contract(d[:, m * shard:(m + 1) * shard], cols[m], ((1,), (1,)))
        unit, _ = units(q)
        tally[0, 0:1] += jnp.sum(total * unit, axis=0, keepdims=True)
        mine[...] = total
        for kind in range(2):
            parts[q, kind] = total[:, kind * (width // 2):(kind + 1) * (width // 2)].astype(low)

        @pl.when(i == 0)
        def _():
            n_copy(0, 1).start()
            n_copy(1, 1).start()
            for m in range(1, 4):
                add_core(m)

        @pl.when(i == 1)
        def _():
            n_copy(1, 0).start()

        @pl.when(i == 2)
        def _():
            n_copy(0, 0).start()
        return carry

    lax.fori_loop(0, 4, back_block, 0)

    def m_copy(stage, k):
        slot = (0, 3, 4)[stage] + k
        peer = (around[k], (e ^ 1, s), (e ^ (2 * (k + 1)), s))[stage]
        return remote(tally.at[stage], tally_got.at[slot], m_send.at[slot], m_recv.at[slot], peer)

    for k in range(3):
        m_copy(0, k).start()

    for kind in range(2):
        n_copy(kind, 1).wait_recv()
        group = 2 - kind
        parts[group, kind] = (parts[group, kind].astype(full) + first_got[kind, 1].astype(full)).astype(low)
        n_copy(kind, 2).start()

    total = tally[0]
    for k in range(3):
        m_copy(0, k).wait_recv()
        total += tally_got[k]
    tally[1] = total
    m_copy(1, 0).start()

    def finish_grad(m):
        block = sums[m, z].astype(full)
        for k in range(1, 4):
            z_copy(m, k).wait_recv()
            block += z_got[k - 1, m].astype(full)
        final[m] = block
        for k in range(3):
            a_copy(m, k).start()
        outs[m][:, aligned(s, shard)] = final[m, aligned(s, slim)]

    finish_grad(0)
    m_copy(1, 0).wait_recv()
    total = total + tally_got[3]
    tally[2] = total
    for k in range(3):
        m_copy(2, k).start()
    for m in range(1, 4):
        finish_grad(m)

    for kind in range(2):
        n_copy(kind, 0).wait_recv()
        n_copy(kind, 2).wait_recv()
        lanes = slice(kind * (width // 2), (kind + 1) * (width // 2))
        mine[:, lanes] += first_got[kind, 0].astype(full) + second_got[kind].astype(full)
    unit, scale = units(0)
    unit_grad = mine[...] * gain
    tokens_grad[...] = residual_grad[...] + scale * (
        unit_grad - unit * jnp.mean(unit_grad * unit, axis=1, keepdims=True)
    )
    for k in range(3):
        m_copy(2, k).wait_recv()
        total += tally_got[4 + k]
    small_sum[...] = total
    for m in range(4):
        core_copy(m).wait_send()
        for k in range(3):
            z_copy(m, k + 1).wait_send()
            a_copy(m, k).wait()
    for kind in range(2):
        for which in range(3):
            n_copy(kind, which).wait_send()
    for stage, amount in ((0, 3), (1, 1), (2, 3)):
        for k in range(amount):
            m_copy(stage, k).wait_send()


def finish_grads(all_tokens, dqkv, cols, att_full, aog_cols, residual_grad, params, small, bias_grad):
    rows, width = residual_grad.shape
    shard = cols.shape[2]
    slim = width // 32
    low, full = jnp.bfloat16, jnp.float32
    vmem = pl.BlockSpec(memory_space=pltpu.VMEM)
    dma = pltpu.SemaphoreType.DMA
    return pl.pallas_call(
        finish_kernel,
        out_shape=(jax.ShapeDtypeStruct((rows, width), full),)
        + (jax.ShapeDtypeStruct((slim, width), full),) * 4
        + (jax.ShapeDtypeStruct((16, width), full),),
        in_specs=[vmem] * 9,
        out_specs=(vmem,) * 6,
        scratch_shapes=[
            pltpu.VMEM((2, 4, 4, shard // 2, shard), low),
            pltpu.VMEM((4, 4, shard // 2, shard), low),
            pltpu.VMEM((4, 4, shard // 2, shard), low),
            pltpu.VMEM((3, 4, shard // 2, shard), low),
            pltpu.VMEM((4, shard // 2, shard), full),
            pltpu.VMEM((4, 2, rows, width // 2), low),
            pltpu.VMEM((2, 2, rows, width // 2), low),
            pltpu.VMEM((2, rows, width // 2), low),
            pltpu.VMEM((rows, width), full),
            pltpu.VMEM((4 * rows, width), low),
            pltpu.VMEM((3, 16, width), full),
            pltpu.VMEM((7, 16, width), full),
            dma((4,)), dma((4,)), dma((4, 3)), dma((4, 3)), dma((4, 3)), dma((4, 3)),
            dma((2, 3)), dma((2, 3)), dma((7,)), dma((7,)),
        ],
        compiler_params=pltpu.CompilerParams(
            collective_id=5, has_side_effects=True, vmem_limit_bytes=VMEM_LIMIT
        ),
        cost_estimate=pl.CostEstimate(flops=60 * rows * width * shard, bytes_accessed=14 << 20, transcendentals=0),
        name="finish_grads",
    )(all_tokens, dqkv, cols, att_full, aog_cols, residual_grad, params, small, bias_grad)


def per_device_kernels(
    tokens, cotangent, expert_ids, segment_lengths, segment_parents, attention_gain,
    query_weight, key_weight, value_weight, output_weight, bias_table, feedforward_gain,
    router_weight, gate_weight, up_weight, down_weight,
):
    place = lax.axis_index(EXPERT) * lax.axis_size(SEQ) + lax.axis_index(SEQ)
    count = lax.axis_size(EXPERT) * lax.axis_size(SEQ)
    rows = tokens.shape[0]
    output_full = lax.all_gather(output_weight, BOTH, axis=0, tiled=True)

    def spread(values):
        length = values.shape[-1]
        lane = jnp.arange(count * length, dtype=jnp.int32) // length
        wide = jnp.where(lane == place, jnp.tile(values, (1, count)), jnp.zeros((), values.dtype))
        return jnp.pad(wide, ((0, 0), (0, D - wide.shape[1])))

    misc = jnp.concatenate([
        spread(attention_gain[None]), spread(feedforward_gain[None]), spread(bias_table[None]),
        jnp.zeros((5, D), jnp.bfloat16), spread(router_weight.T),
    ], axis=0)
    all_tokens, qkv, cols, params = project(tokens, query_weight, key_weight, value_weight, misc)
    attended = attend(segment_lengths, segment_parents, qkv, params)
    attended_full = lax.all_gather(attended, SEQ, axis=1, tiled=True)
    ids_row = expert_ids.T
    send_rows, grad_rows, residual = dispatch(
        attended, output_full, tokens, cotangent, params, expert_ids, ids_row
    )
    returned, grad_back, gate_term, up_term, down_term = experts(
        send_rows, grad_rows, gate_weight[0], up_weight[0], down_weight[0]
    )
    layer_out, residual_grad, attended_grad, out_grad_cols, small = combine(
        returned, grad_back, residual, cotangent, output_full, params, expert_ids, ids_row
    )
    dqkv, bias_grad = attend_back(segment_lengths, segment_parents, qkv, params, attended_grad)
    tokens_grad, dwq, dwk, dwv, dwo, totals = finish_grads(
        all_tokens, dqkv, cols, attended_full, out_grad_cols, residual_grad, params, small, bias_grad
    )

    def own(values, length):
        return lax.dynamic_slice_in_dim(values, place * length, length, values.ndim - 1)

    slim = D // count
    return (
        layer_out,
        tokens_grad,
        own(totals[0], slim),
        dwq,
        dwk,
        dwv,
        dwo,
        own(totals[2], BUCKETS * HEADS // count),
        own(totals[1], slim),
        own(totals[8:16], slim).T,
        gate_term[None],
        up_term[None],
        down_term[None],
        jnp.sqrt(totals[3, 0:2] / (rows * count * D)),
    )


def per_device_general(
    tokens,
    cotangent,
    expert_ids,
    segment_lengths,
    segment_parents,
    attention_gain,
    query_weight,
    key_weight,
    value_weight,
    output_weight,
    bias_table,
    feedforward_gain,
    router_weight,
    gate_weight,
    up_weight,
    down_weight,
):
    seq_count = lax.axis_size(SEQ)
    seq_place = lax.axis_index(SEQ)
    all_count = lax.axis_size(EXPERT) * seq_count
    row_count = tokens.shape[0]
    experts = lax.axis_size(EXPERT) * gate_weight.shape[0]
    capacity = 10 * row_count // (4 * experts)
    score_scale = HDIM ** (-0.5)
    gathered = (
        lax.all_gather(attention_gain, BOTH, axis=0, tiled=True),
        lax.all_gather(query_weight, BOTH, axis=0, tiled=True),
        lax.all_gather(key_weight, BOTH, axis=0, tiled=True),
        lax.all_gather(value_weight, BOTH, axis=0, tiled=True),
        lax.all_gather(output_weight, BOTH, axis=0, tiled=True),
        lax.all_gather(bias_table, BOTH, axis=0, tiled=True),
        lax.all_gather(feedforward_gain, BOTH, axis=0, tiled=True),
        lax.all_gather(router_weight, BOTH, axis=0, tiled=True),
    )
    gain_one, query_full, key_full, value_full, output_full, bias_flat, gain_two, router_full = (
        gathered
    )
    bias_grid = bias_flat.reshape(BUCKETS, HEADS)
    starts, before, reaches = tree_tables(segment_lengths[0], segment_parents[0])
    own_rows = seq_place * row_count + jnp.arange(row_count, dtype=jnp.int32)
    own_meta = token_info(own_rows, starts, before, reaches)
    tokens_float = tokens.astype(jnp.float32)
    scale_one = norm_factor(tokens_float)
    unit_one = tokens_float * scale_one
    normed_one = (unit_one * gain_one.astype(jnp.float32)).astype(jnp.bfloat16)
    queries = (
        jnp.dot(normed_one, query_full, preferred_element_type=jnp.float32)
        .astype(jnp.bfloat16)
        .reshape(row_count, HEADS, HDIM)
    )
    keys_own = (
        jnp.dot(normed_one, key_full, preferred_element_type=jnp.float32)
        .astype(jnp.bfloat16)
        .reshape(row_count, HEADS, HDIM)
    )
    values_own = (
        jnp.dot(normed_one, value_full, preferred_element_type=jnp.float32)
        .astype(jnp.bfloat16)
        .reshape(row_count, HEADS, HDIM)
    )
    row_peak = jnp.full((HEADS, row_count), NEGATIVE, jnp.float32)
    key_piece = lax.all_gather(keys_own, SEQ, axis=0, tiled=True)
    value_piece = lax.all_gather(values_own, SEQ, axis=0, tiled=True)
    key_rows = jnp.arange(key_piece.shape[0], dtype=jnp.int32)
    visible, onehot, pair_bias = pair_terms(
        own_meta, token_info(key_rows, starts, before, reaches), own_rows, key_rows, bias_grid
    )
    scores = masked_scores(queries, key_piece, visible, pair_bias)
    new_peak = jnp.maximum(row_peak, jnp.max(scores, axis=-1))
    expo = jnp.exp(scores - new_peak[:, :, None])
    row_total = jnp.sum(expo, axis=-1)
    summed = jnp.einsum(
        SPEC_2, expo.astype(jnp.bfloat16), value_piece, preferred_element_type=jnp.float32
    )
    row_peak, row_total, summed = (new_peak, row_total, summed)
    log_total = row_peak + jnp.log(row_total)
    attended_float = summed / jnp.transpose(row_total)[:, :, None]
    attended = attended_float.astype(jnp.bfloat16).reshape(row_count, D)
    residual = tokens_float + jnp.dot(attended, output_full, preferred_element_type=jnp.float32)
    scale_two = norm_factor(residual)
    unit_two = residual * scale_two
    normed_two = (unit_two * gain_two.astype(jnp.float32)).astype(jnp.bfloat16)
    router_prob = jax.nn.softmax(
        jnp.dot(normed_two, router_full, preferred_element_type=jnp.float32), axis=-1
    )
    pick_hot = (
        expert_ids[:, :, None] == jnp.arange(experts, dtype=jnp.int32)[None, None, :]
    ).astype(jnp.float32)
    chosen = jnp.sum(pick_hot * router_prob[:, None, :], axis=2)
    chosen_total = jnp.sum(chosen, axis=1, keepdims=True)
    gate_shares = chosen / chosen_total
    hot_int = pick_hot.astype(jnp.int32).reshape(row_count * 2, experts)
    earlier = jnp.cumsum(hot_int, axis=0) - hot_int
    slot_number = jnp.sum(earlier * hot_int, axis=1).reshape(row_count, 2)
    kept_copy = slot_number < capacity
    kept_float = kept_copy.astype(jnp.float32)
    target = jnp.where(kept_copy, expert_ids * capacity + slot_number, experts * capacity)
    copy_ids = jnp.arange(row_count * 2, dtype=jnp.int32)
    slot_copy = (
        jnp.full((experts * capacity + 1,), row_count * 2, jnp.int32)
        .at[target.reshape(-1)]
        .set(copy_ids)[: experts * capacity]
    )
    fetch_index = jnp.minimum(target, experts * capacity - 1).reshape(-1)
    token_of_slot = jnp.where(slot_copy < row_count * 2, slot_copy // 2, row_count)
    padded = jnp.concatenate([normed_two, jnp.zeros((1, D), jnp.bfloat16)], axis=0)
    send_rows = padded[token_of_slot].reshape(experts, capacity, D)
    expert_in = lax.all_to_all(send_rows, EXPERT, split_axis=0, concat_axis=1, tiled=True)[0]
    gate_piece = lax.all_gather(gate_weight, SEQ, axis=1, tiled=True)
    up_piece = lax.all_gather(up_weight, SEQ, axis=1, tiled=True)
    down_piece = lax.all_gather(down_weight, SEQ, axis=1, tiled=True)
    gate_pre = jnp.einsum(SPEC_3, expert_in, gate_piece[0], preferred_element_type=jnp.float32)
    up_pre = jnp.einsum(SPEC_3, expert_in, up_piece[0], preferred_element_type=jnp.float32)
    active = (gelu_tanh(gate_pre) * up_pre).astype(jnp.bfloat16)
    expert_sum = jnp.dot(active, down_piece[0], preferred_element_type=jnp.float32)
    returned = lax.all_to_all(
        expert_sum.astype(jnp.bfloat16)[None], EXPERT, split_axis=1, concat_axis=0, tiled=True
    )
    picked = (
        returned.reshape(experts * capacity, D)[fetch_index]
        .reshape(row_count, 2, D)
        .astype(jnp.float32)
    )
    weighted = gate_shares * kept_float
    mixture = jnp.sum(weighted[:, :, None] * picked, axis=1)
    layer_out = (residual + mixture).astype(jnp.bfloat16)
    local_sums = jnp.stack([jnp.sum(residual * residual), jnp.sum(mixture * mixture)])
    again = (
        lax.all_gather(attention_gain, BOTH, axis=0, tiled=True),
        lax.all_gather(query_weight, BOTH, axis=0, tiled=True),
        lax.all_gather(key_weight, BOTH, axis=0, tiled=True),
        lax.all_gather(value_weight, BOTH, axis=0, tiled=True),
        lax.all_gather(output_weight, BOTH, axis=0, tiled=True),
        lax.all_gather(bias_table, BOTH, axis=0, tiled=True),
        lax.all_gather(feedforward_gain, BOTH, axis=0, tiled=True),
        lax.all_gather(router_weight, BOTH, axis=0, tiled=True),
    )
    gain_one, query_full, key_full, value_full, output_full, bias_flat, gain_two, router_full = (
        again
    )
    bias_grid = bias_flat.reshape(BUCKETS, HEADS)
    grad_out = cotangent.astype(jnp.float32)
    copy_grad = (
        (weighted[:, :, None] * grad_out[:, None, :]).astype(jnp.bfloat16).reshape(row_count * 2, D)
    )
    copy_padded = jnp.concatenate([copy_grad, jnp.zeros((1, D), jnp.bfloat16)], axis=0)
    grad_send = copy_padded[slot_copy].reshape(experts, capacity, D)
    grad_in = lax.all_to_all(grad_send, EXPERT, split_axis=0, concat_axis=1, tiled=True)[0]
    gate_piece = lax.all_gather(gate_weight, SEQ, axis=1, tiled=True)
    up_piece = lax.all_gather(up_weight, SEQ, axis=1, tiled=True)
    down_piece = lax.all_gather(down_weight, SEQ, axis=1, tiled=True)
    gate_pre = jnp.einsum(SPEC_3, expert_in, gate_piece[0], preferred_element_type=jnp.float32)
    up_pre = jnp.einsum(SPEC_3, expert_in, up_piece[0], preferred_element_type=jnp.float32)
    gelu_out, gelu_pull = jax.vjp(gelu_tanh, gate_pre)
    act_grad = jnp.einsum(SPEC_3, grad_in, down_piece[0], preferred_element_type=jnp.float32)
    gate_back = gelu_pull(act_grad * up_pre)[0].astype(jnp.bfloat16)
    up_back = (act_grad * gelu_out).astype(jnp.bfloat16)
    input_grad = jnp.dot(gate_back, gate_piece[0], preferred_element_type=jnp.float32) + jnp.dot(
        up_back, up_piece[0], preferred_element_type=jnp.float32
    )
    active = (gelu_out * up_pre).astype(jnp.bfloat16)
    input_grad, gate_backs, up_backs, actives = (input_grad, gate_back, up_back, active)
    grad_back = lax.all_to_all(
        input_grad.astype(jnp.bfloat16)[None], EXPERT, split_axis=1, concat_axis=0, tiled=True
    )
    expert_back = (
        grad_back.reshape(experts * capacity, D)[fetch_index]
        .reshape(row_count, 2, D)
        .astype(jnp.float32)
    )
    normed_two_grad = jnp.sum(expert_back * kept_float[:, :, None], axis=1)
    expert_grads = lax.psum_scatter(
        jnp.stack(
            [
                jnp.einsum(SPEC_4, gate_backs, expert_in, preferred_element_type=jnp.float32),
                jnp.einsum(SPEC_4, up_backs, expert_in, preferred_element_type=jnp.float32),
                jnp.einsum(SPEC_4, actives, grad_in, preferred_element_type=jnp.float32),
            ],
            axis=1,
        ).astype(jnp.bfloat16),
        SEQ,
        scatter_dimension=0,
        tiled=True,
    ).astype(jnp.float32)
    share_grad = jnp.sum(grad_out[:, None, :] * picked, axis=2) * kept_float
    chosen_grad = (
        share_grad - jnp.sum(gate_shares * share_grad, axis=1, keepdims=True)
    ) / chosen_total
    prob_grad = jnp.sum(pick_hot * chosen_grad[:, :, None], axis=1)
    logit_grad = router_prob * (prob_grad - jnp.sum(router_prob * prob_grad, axis=1, keepdims=True))
    router_float = router_full.astype(jnp.float32)
    router_term = jnp.einsum(
        SPEC_5, normed_two.astype(jnp.float32), logit_grad, precision=lax.Precision.HIGHEST
    )
    normed_two_grad = normed_two_grad + jnp.einsum(
        SPEC_6, logit_grad, router_float, precision=lax.Precision.HIGHEST
    )
    gain_two_term = jnp.sum(normed_two_grad * unit_two, axis=0)
    unit_grad_two = normed_two_grad * gain_two.astype(jnp.float32)
    residual_grad = grad_out + scale_two * (
        unit_grad_two - unit_two * jnp.mean(unit_grad_two * unit_two, axis=-1, keepdims=True)
    )
    attention_out_grad = residual_grad.astype(jnp.bfloat16)
    output_term = jnp.einsum(
        SPEC_5, attended, attention_out_grad, preferred_element_type=jnp.float32
    )
    attended_grad = (
        jnp.einsum(SPEC_6, attention_out_grad, output_full, preferred_element_type=jnp.float32)
        .astype(jnp.bfloat16)
        .reshape(row_count, HEADS, HDIM)
    )
    row_delta = jnp.transpose(jnp.sum(attended_grad.astype(jnp.float32) * attended_float, axis=-1))
    total_all, delta_all = (
        lax.all_gather(log_total, SEQ, axis=1, tiled=True),
        lax.all_gather(row_delta, SEQ, axis=1, tiled=True),
    )
    key_piece = lax.all_gather(keys_own, SEQ, axis=0, tiled=True)
    value_piece = lax.all_gather(values_own, SEQ, axis=0, tiled=True)
    key_rows = jnp.arange(key_piece.shape[0], dtype=jnp.int32)
    visible, onehot, pair_bias = pair_terms(
        own_meta, token_info(key_rows, starts, before, reaches), own_rows, key_rows, bias_grid
    )
    scores = masked_scores(queries, key_piece, visible, pair_bias)
    soft_weights = jnp.exp(scores - log_total[:, :, None])
    dprob = jnp.einsum(
        SPEC_1, attended_grad, value_piece, preferred_element_type=jnp.float32
    )
    score_grad = (soft_weights * (dprob - row_delta[:, :, None])).astype(jnp.bfloat16)
    query_acc = jnp.einsum(
        SPEC_2, score_grad, key_piece, preferred_element_type=jnp.float32
    )
    bias_acc = jnp.einsum(SPEC_7, onehot, score_grad, preferred_element_type=jnp.float32)
    query_acc, bias_acc = (query_acc, bias_acc)
    query_piece = lax.all_gather(queries, SEQ, axis=0, tiled=True)
    grad_piece = lax.all_gather(attended_grad, SEQ, axis=0, tiled=True)
    piece_rows = query_piece.shape[0]
    query_rows = jnp.arange(piece_rows, dtype=jnp.int32)
    visible, onehot, pair_bias = pair_terms(
        token_info(query_rows, starts, before, reaches), own_meta, query_rows, own_rows, bias_grid
    )
    scores = masked_scores(query_piece, keys_own, visible, pair_bias)
    soft_weights = jnp.exp(scores - total_all[:, :, None])
    value_acc = jnp.einsum(
        SPEC_8,
        soft_weights.astype(jnp.bfloat16),
        grad_piece,
        preferred_element_type=jnp.float32,
    )
    dprob = jnp.einsum(SPEC_1, grad_piece, values_own, preferred_element_type=jnp.float32)
    score_grad = (soft_weights * (dprob - delta_all[:, :, None])).astype(jnp.bfloat16)
    key_acc = jnp.einsum(
        SPEC_8, score_grad, query_piece, preferred_element_type=jnp.float32
    )
    key_acc, value_acc = (key_acc, value_acc)
    query_back = (query_acc * score_scale).astype(jnp.bfloat16).reshape(row_count, D)
    key_back = (key_acc * score_scale).astype(jnp.bfloat16).reshape(row_count, D)
    value_back = value_acc.astype(jnp.bfloat16).reshape(row_count, D)
    query_term = jnp.einsum(SPEC_5, normed_one, query_back, preferred_element_type=jnp.float32)
    key_term = jnp.einsum(SPEC_5, normed_one, key_back, preferred_element_type=jnp.float32)
    value_term = jnp.einsum(SPEC_5, normed_one, value_back, preferred_element_type=jnp.float32)
    normed_one_grad = jnp.einsum(
        SPEC_6, query_back, query_full, preferred_element_type=jnp.float32
    )
    normed_one_grad = normed_one_grad + jnp.einsum(
        SPEC_6, key_back, key_full, preferred_element_type=jnp.float32
    )
    normed_one_grad = normed_one_grad + jnp.einsum(
        SPEC_6, value_back, value_full, preferred_element_type=jnp.float32
    )
    gain_one_term = jnp.sum(normed_one_grad * unit_one, axis=0)
    unit_grad_one = normed_one_grad * gain_one.astype(jnp.float32)
    tokens_grad = residual_grad + scale_one * (
        unit_grad_one - unit_one * jnp.mean(unit_grad_one * unit_one, axis=-1, keepdims=True)
    )
    stats_term = jnp.broadcast_to(local_sums[None, :], (all_count, 2))
    reduced = (
        lax.psum_scatter(gain_one_term, BOTH, scatter_dimension=0, tiled=True),
        lax.psum_scatter(query_term, BOTH, scatter_dimension=0, tiled=True),
        lax.psum_scatter(key_term, BOTH, scatter_dimension=0, tiled=True),
        lax.psum_scatter(value_term, BOTH, scatter_dimension=0, tiled=True),
        lax.psum_scatter(output_term, BOTH, scatter_dimension=0, tiled=True),
        lax.psum_scatter(
            bias_acc.reshape(BUCKETS * HEADS), BOTH, scatter_dimension=0, tiled=True
        ),
        lax.psum_scatter(gain_two_term, BOTH, scatter_dimension=0, tiled=True),
        lax.psum_scatter(router_term, BOTH, scatter_dimension=0, tiled=True),
        lax.psum_scatter(stats_term, BOTH, scatter_dimension=0, tiled=True),
    )
    roots = jnp.sqrt(reduced[8][0] / (row_count * all_count * D))
    return (
        layer_out,
        tokens_grad,
        reduced[0],
        reduced[1],
        reduced[2],
        reduced[3],
        reduced[4],
        reduced[5],
        reduced[6],
        reduced[7],
        expert_grads[None, :, 0, :],
        expert_grads[None, :, 1, :],
        expert_grads[None, :, 2, :],
        roots,
    )


def solution(mesh):
    kernels_fit = mesh.shape[EXPERT] == len(ORDER) and mesh.shape[SEQ] == 4
    return jax.shard_map(
        per_device_kernels if kernels_fit else per_device_general,
        mesh=mesh,
        in_specs=(
            P(BOTH, None),
            P(BOTH, None),
            P(BOTH, None),
            P(EXPERT, None),
            P(EXPERT, None),
            P(BOTH),
            P(BOTH, None),
            P(BOTH, None),
            P(BOTH, None),
            P(BOTH, None),
            P(BOTH),
            P(BOTH),
            P(BOTH, None),
            P(EXPERT, SEQ, None),
            P(EXPERT, SEQ, None),
            P(EXPERT, SEQ, None),
        ),
        out_specs=(
            P(BOTH, None),
            P(BOTH, None),
            P(BOTH),
            P(BOTH, None),
            P(BOTH, None),
            P(BOTH, None),
            P(BOTH, None),
            P(BOTH),
            P(BOTH),
            P(BOTH, None),
            P(EXPERT, SEQ, None),
            P(EXPERT, SEQ, None),
            P(EXPERT, SEQ, None),
            P(),
        ),
        check_vma=False,
    )
```

time: 1580 us -> 449 us (0.28)
  waiting for transfers between devices: 936 us -> 9.15 us
  Pallas kernels: 0 us -> 394 us
  matrix products: 226 us -> 0 us
  blocking collectives: 163 us -> 0 us
  local copies, waits for them, and re-layouts: 127 us -> 22.1 us
  other arithmetic: 84.8 us -> 1.25 us
  starting transfers between devices: 18.1 us -> 0.08 us
    reduce_scatter x5 -> x0, waiting for transfers between devices: 674 us -> none  [the longest x1 143 us: per_device(): lax.psum_scatter(value_term, ('expert', 'seq'), scatter_dimension=0, tile...]
    pallas_call x0 -> x7, Pallas kernels: none -> 394 us  [the longest x1 223 us: experts(): pl.pallas_call(expert_kernel, out_shape=(jax.ShapeDtypeStruct((rows, widt...]
    dot_general x35 -> x0, matrix products: 224 us -> none  [the longest x2 46.3 us: masked_scores(): jnp.einsum('qhd,khd->hqk', query_block, key_block, preferred_element_type...]
    all_gather x11 -> x2, waiting for transfers between devices: 197 us -> 8.46 us  [the longest x1 8.45 us: per_device_kernels(): output_full = lax.all_gather(output_weight, BOTH, axis=0, tiled=True)]
    all_gather x3 -> x0, blocking collectives: 83.5 us -> none  [the longest x1 67.3 us: per_device(): lax.all_gather(router_weight, ('expert', 'seq'), axis=0, tiled=True)]
    unnamed x2 -> x0, blocking collectives: 80 us -> none
    all_to_all x4 -> x0, waiting for transfers between devices: 47.6 us -> none  [the longest x1 28.7 us: per_device(): lax.all_to_all(grad_send, 'expert', split_axis=0, concat_axis=1, tiled=True)]
    eq x3 -> x0, local copies, waits for them, and re-layouts: 46.9 us -> none  [the longest x1 46.6 us: pair_terms(): bucket_of(distance)[:, :, None]]
  transfers between devices with their start and end apart: 21 -> 2, of which waited for: 14 -> 1; matrix products, arithmetic and copies ran while one was open for 25% -> 1% of each run, Pallas kernels for 0% -> 80%
where the time goes in v1:
time: 449 us; the launch traced here: 441 us
  Pallas kernels  394 us (88%)
  local copies, waits for them, and re-layouts  22.1 us (5%)
  between operations  14.6 us (3%)
  waiting for transfers between devices  9.15 us (2%)
    pallas_call x1, Pallas kernels, experts(): pl.pallas_call(expert_kernel, out_shape=(jax.ShapeDtypeStruct((rows, widt...  223 us
    pallas_call x1, Pallas kernels, finish_grads(): pl.pallas_call(finish_kernel, out_shape=(jax.ShapeDtypeStruct((rows, widt...  42.7 us
    pallas_call x1, Pallas kernels, project(): pl.pallas_call(project_kernel, out_shape=(jax.ShapeDtypeStruct((4 * rows,...  36.9 us
    pallas_call x1, Pallas kernels, attend_back(): pl.pallas_call(attend_back_kernel, out_shape=(jax.ShapeDtypeStruct((total...  31.9 us
    pallas_call x1, Pallas kernels, combine(): pl.pallas_call(combine_kernel, out_shape=(jax.ShapeDtypeStruct((rows, wid...  23.9 us
    pallas_call x1, Pallas kernels, attend(): pl.pallas_call(attend_kernel, out_shape=jax.ShapeDtypeStruct((total, shar...  19.1 us
    pallas_call x1, Pallas kernels, dispatch(): pl.pallas_call(dispatch_kernel, out_shape=(jax.ShapeDtypeStruct((8 * cap,...  15.6 us
    unnamed x28, local copies, waits for them, and re-layouts  13.7 us
  transfers between devices with their start and end apart: 2, of which 1 were waited for; matrix products, arithmetic and copies ran while one was open for 1% of the time, Pallas kernels for 80%

profile of v1, /device:TPU:0, one launch (start us, length us, event | category | flops | bytes accessed | tf_op | source)
XLA Modules:
  0.0 440.9 jit_solution(3505088966155050528)
XLA Ops:
  7.2 0.7 all-gather.3.cloned.1.call-update
  8.0 0.7 tile.16
  8.7 0.7 tile.35
  9.5 0.7 tile.39
  10.3 0.7 tile.37
  11.1 1.2 concatenate.3.misc
  12.4 36.9 %project.1 = (bf16[1024,1024]{1,0:T(8,128)(2,1)}, bf16[1024,768]{1,0:T(8,128)(2,1)}, bf16[3,1024,256]{2,1,0:T(8,128)(2,1)}, f32[16,1024]{1,0:T(8,128)}) custom-call(bf16[256,1024]{1,0:T(8,128)(2,1)} %tokens.3, bf16[32,1024]{1,0:T(8,128)(2,1)} %wq.1, bf16[32,1024]{1,0:T(8,128)(2,1)} %wk.1, bf16[32,1024]{1,0:T(8,128)(2,1)} %wv.1, bf16[16,1024]{1,0:T(8,128)(2,1)} %concatenate.3.misc), custom_call_target="tpu_custom_call" | custom-call | flops 1610612736 | bytes 10485760 | tf_op jit(solution)/shard_map/project/pallas_call | solution.py:518
  49.3 19.1 %attend.1.att = bf16[1024,256]{1,0:T(8,128)(2,1)} custom-call(s32[1,13]{1,0:T(1,128)} %lengths.3, s32[1,13]{1,0:T(1,128)} %parents.3, bf16[1024,768]{1,0:T(8,128)(2,1)} %get-tuple-element.39.qkv, f32[16,1024]{1,0:T(8,128)} %get-tuple-element.40.params), custom_call_target="tpu_custom_call" | custom-call | flops 1073741824 | bytes 4194304 | tf_op jit(solution)/shard_map/attend/pallas_call | solution.py:646
  68.5 0.8 copy.32.ids
  69.3 8.5 %all-gather.3.cloned.1.call-done.wo = bf16[1024,1024]{1,0:T(8,128)(2,1)} async-done(((bf16[32,1024]{1,0:T(8,128)(2,1)}), bf16[1024,1024]{1,0:T(8,128)(2,1)}) %all-gather.3.cloned.1.call-update) | async-done | bytes 2097168 | tf_op jit(solution)/shard_map/all_gather | solution.py:1173
  77.8 15.6 %dispatch.1 = (bf16[640,1024]{1,0:T(8,128)(2,1)}, bf16[640,1024]{1,0:T(8,128)(2,1)}, f32[256,1024]{1,0:T(8,128)}) custom-call(bf16[1024,256]{1,0:T(8,128)(2,1)} %attend.1.att, bf16[1024,1024]{1,0:T(8,128)(2,1)} %all-gather.3.cloned.1.call-done.wo, bf16[256,1024]{1,0:T(8,128)(2,1)} %tokens.3, bf16[256,1024]{1,0:T(8,128)(2,1)} %cotangent.3, ...), custom_call_target="tpu_custom_call" | custom-call | flops 1610612736 | bytes 8388608 | tf_op jit(solution)/shard_map/dispatch/pallas_call | solution.py:843
  93.4 223.5 %experts.1 = (bf16[640,1024]{1,0:T(8,128)(2,1)}, bf16[640,1024]{1,0:T(8,128)(2,1)}, f32[704,1024]{1,0:T(8,128)}, f32[704,1024]{1,0:T(8,128)}, f32[704,1024]{1,0:T(8,128)}) custom-call(bf16[640,1024]{1,0:T(8,128)(2,1)} %get-tuple-element.41.xs, bf16[640,1024]{1,0:T(8,128)(2,1)} %get-tuple-element.42.gs, bf16[704,1024]{1,0:T(8,128)(2,1)} %bitcast.24, ...), custom_call_target="tpu_custom_call" | custom-call | flops 33218887680 | bytes 20971520 | tf_op jit(solution)/shard_map/experts/pallas_call | solution.py:339
  316.9 23.9 %combine.1 = (bf16[256,1024]{1,0:T(8,128)(2,1)}, f32[256,1024]{1,0:T(8,128)}, bf16[1024,256]{1,0:T(8,128)(2,1)}, bf16[1024,256]{1,0:T(8,128)(2,1)}, f32[16,1024]{1,0:T(8,128)}) custom-call(bf16[640,1024]{1,0:T(8,128)(2,1)} %get-tuple-element.43.ret_o, bf16[640,1024]{1,0:T(8,128)(2,1)} %get-tuple-element.44.ret_b, f32[256,1024]{1,0:T(8,128)} %get-tuple-element.45.residual, ...), custom_call_target="tpu_custom_call" | custom-call | flops 1610612736 | bytes 12582912 | tf_op jit(solution)/shard_map/combine/pallas_call | solution.py:929
  340.8 31.9 %attend_back.1 = (bf16[1024,768]{1,0:T(8,128)(2,1)}, f32[8,512]{1,0:T(8,128)}) custom-call(s32[1,13]{1,0:T(1,128)} %lengths.3, s32[1,13]{1,0:T(1,128)} %parents.3, bf16[1024,768]{1,0:T(8,128)(2,1)} %get-tuple-element.39.qkv, f32[16,1024]{1,0:T(8,128)} %get-tuple-element.40.params, bf16[1024,256]{1,0:T(8,128)(2,1)} %get-tuple-element.48.grad), custom_call_target="tpu_custom_call" | custom-call | flops 2684354560 | bytes 6291456 | tf_op jit(solution)/shard_map/attend_back/pallas_call | solution.py:749
  372.7 42.7 %finish_grads.1 = (f32[256,1024]{1,0:T(8,128)}, f32[32,1024]{1,0:T(8,128)}, f32[32,1024]{1,0:T(8,128)}, f32[32,1024]{1,0:T(8,128)}, f32[32,1024]{1,0:T(8,128)}, /*index=5*/f32[16,1024]{1,0:T(8,128)}) custom-call(bf16[1024,1024]{1,0:T(8,128)(2,1)} %get-tuple-element.47.all_tokens, bf16[1024,768]{1,0:T(8,128)(2,1)} %get-tuple-element.49.dqkv, ...), custom_call_target="tpu_custom_call" | custom-call | flops 4026531840 | bytes 14680064 | tf_op jit(solution)/shard_map/finish_grads/pallas_call | solution.py:1134
  415.4 0.8 slice.18
  416.3 0.9 fusion.7
  417.1 1.2 sqrt_bitcast_fusion
  418.4 0.7 dynamic-slice_bitcast_fusion
  419.0 0.6 fusion.4
  419.6 0.6 fusion.6
  420.8 0.8 copy.43
  421.6 1.0 copy.44
  422.5 1.8 copy.45
  424.4 0.7 copy.46
  425.0 0.7 copy.47
  425.7 0.7 copy.48
  426.4 1.6 copy.49
  427.9 1.3 copy-done.1
  429.2 1.6 copy.50
  430.8 1.3 copy-done
  432.1 1.6 copy.51
  (31 shorter events, 1.2 us)
Async XLA Ops:
  7.2 70.6 %all-gather.3.cloned.1.call-start = ((), (), s32[]{:S(2)}) async-start(), calls=%async_computation | async-start | bytes 2162688 | tf_op jit(solution)/shard_map/all_gather | solution.py:1173
  7.9 364.8 %all-gather.5.cloned.1.call-start = ((), (), s32[]{:S(2)}) async-start(), calls=%async_computation.1 | async-start | bytes 2621440 | tf_op jit(solution)/shard_map/all_gather | solution.py:1187
  49.3 19.2 %copy-start.8 = (s32[256,2]{0,1:T(2,128)S(1)}, s32[256,2]{0,1:T(2,128)}, u32[]{:S(2)}) copy-start(s32[256,2]{0,1:T(2,128)} %param.18) | copy-start | bytes 6148
  372.7 48.1 %copy-start.4 = (bf16[256,1024]{1,0:T(8,128)(2,1)S(1)}, bf16[256,1024]{1,0:T(8,128)(2,1)}, u32[]{:S(2)}) copy-start(bf16[256,1024]{1,0:T(8,128)(2,1)} %get-tuple-element.83) | copy-start | bytes 1572868
  415.4 6.2 %copy-start.3 = (f32[256,1024]{1,0:T(8,128)S(1)}, f32[256,1024]{1,0:T(8,128)}, u32[]{:S(2)}) copy-start(f32[256,1024]{1,0:T(8,128)} %get-tuple-element.84) | copy-start | bytes 3145732
  420.8 3.6 copy-start.7
  420.8 4.3 copy-start.6
  420.8 4.9 %copy-start.5 = (f32[32,1024]{1,0:T(8,128)S(1)}, f32[32,1024]{1,0:T(8,128)}, u32[]{:S(2)}) copy-start(f32[32,1024]{1,0:T(8,128)} %get-tuple-element.89) | copy-start | bytes 393220
  421.6 4.8 %copy-start.2 = (f32[704,1024]{1,0:T(8,128)S(1)}, f32[704,1024]{1,0:T(8,128)}, u32[]{:S(2)}) copy-start(f32[704,1024]{1,0:T(8,128)} %get-tuple-element.61) | copy-start | bytes 8650756
  426.4 2.9 copy-start.1
  429.2 2.9 copy-start
Sparse Core Ops, SparseCore 0:
  10.9 66.8 all-gather.2
  80.2 45.2 all-gather.4
